TPU v7x, 32 devices: a whole 2x2x4 slice. The times are simulated.
32 devices in a mesh: section: 8 (over y, x, core), dp: 4 (over z).
Axes of the slice: x: 2, y: 2, z: 4, core: 2. Of those that a mesh axis runs over, the one named last changes fastest.
Arguments:
- tokens: bfloat16 [16, 32, 1024], P('dp'), may hold values from -6 to 6
- cotangent: bfloat16 [16, 32, 1024], P('dp'), may hold values from -6 to 6
- lengths: int32 [16, 4], P('dp'), may hold values from 1 to 16, 32 in all within a row
- mixer_gain: bfloat16 [16, 1024], P('section', 'dp'), may hold values from 0.5 to 1.5
- mixer_shift: bfloat16 [16, 1024], P('section', 'dp'), may hold values from -1.75 to 1.75
- input_weight: bfloat16 [16, 1024, 3072], P('section', 'dp'), may hold values from -0.1875 to 0.1875
- input_bias: bfloat16 [16, 3072], P('section', 'dp'), may hold values from -1.75 to 1.75
- short_kernel: bfloat16 [16, 3, 3072], P('section', None, 'dp'), may hold values from -3.5 to 3.5
- embed_weight: bfloat16 [16, 33, 64], P('section', None, 'dp'), may hold values from -1 to 1
- embed_bias: bfloat16 [16, 64], P('section', 'dp'), may hold values from -3.140625 to 3.140625
- filter_weight: bfloat16 [16, 64, 64], P('section', None, 'dp'), may hold values from -0.75 to 0.75
- filter_bias: bfloat16 [16, 64], P('section', 'dp'), may hold values from -3.140625 to 3.140625
- taps_weight: bfloat16 [16, 64, 1024], P('section', None, 'dp'), may hold values from -0.75 to 0.75
- skip_gain: bfloat16 [16, 1024], P('section', 'dp'), may hold values from -6 to 6
- output_weight: bfloat16 [16, 1024, 1024], P('section', 'dp'), may hold values from -0.09375 to 0.09375
- output_bias: bfloat16 [16, 1024], P('section', 'dp'), may hold values from -1.75 to 1.75
- feed_gain: bfloat16 [16, 1024], P('section', 'dp'), may hold values from 0.5 to 1.5
- feed_shift: bfloat16 [16, 1024], P('section', 'dp'), may hold values from -1.75 to 1.75
- up_weight: bfloat16 [16, 1024, 4096], P('section', 'dp'), may hold values from -0.1875 to 0.1875
- up_bias: bfloat16 [16, 4096], P('section', 'dp'), may hold values from -1.75 to 1.75
- down_weight: bfloat16 [16, 4096, 1024], P('section', 'dp'), may hold values from -0.09375 to 0.09375
- down_bias: bfloat16 [16, 1024], P('section', 'dp'), may hold values from -1.75 to 1.75
Outputs:
- section_out: float32 [8, 16, 32, 1024], P('section', 'dp')
- section_grad: float32 [8, 16, 32, 1024], P('section', 'dp')
- grad_mixer_gain: float32 [16, 1024], P('section', 'dp')
- grad_mixer_shift: float32 [16, 1024], P('section', 'dp')
- grad_input_weight: float32 [16, 1024, 3072], P('section', 'dp')
- grad_input_bias: float32 [16, 3072], P('section', 'dp')
- grad_short_kernel: float32 [16, 3, 3072], P('section', None, 'dp')
- grad_embed_weight: float32 [16, 33, 64], P('section', None, 'dp')
- grad_embed_bias: float32 [16, 64], P('section', 'dp')
- grad_filter_weight: float32 [16, 64, 64], P('section', None, 'dp')
- grad_filter_bias: float32 [16, 64], P('section', 'dp')
- grad_taps_weight: float32 [16, 64, 1024], P('section', None, 'dp')
- grad_skip_gain: float32 [16, 1024], P('section', 'dp')
- grad_output_weight: float32 [16, 1024, 1024], P('section', 'dp')
- grad_output_bias: float32 [16, 1024], P('section', 'dp')
- grad_feed_gain: float32 [16, 1024], P('section', 'dp')
- grad_feed_shift: float32 [16, 1024], P('section', 'dp')
- grad_up_weight: float32 [16, 1024, 4096], P('section', 'dp')
- grad_up_bias: float32 [16, 4096], P('section', 'dp')
- grad_down_weight: float32 [16, 4096, 1024], P('section', 'dp')
- grad_down_bias: float32 [16, 1024], P('section', 'dp')
Inputs may be any that keep to these rules, and one draw needn't show every extreme that they name: Each row of lengths holds the lengths of 4 documents packed in order into one row of 32 tokens; they sum to 32, and some document in each row has 16 tokens.
All inputs are finite; a program needn't handle non-finite values.
Results may differ from a plain program's by a relative error of at most 0.033.
Values may be sent and summed in bfloat16 or wider, within the bound.
A program may use at most 256 MiB of HBM per device.

v0:
```python
import math

import jax
import jax.numpy as jnp
from jax import lax
from jax.sharding import PartitionSpec as P

EPSILON = 1e-05
MATRICES = (2, 11, 15, 17)


def from_behind(value, axis, steps):
    count = lax.axis_size(axis)
    initial, last = (max(0, -steps), min(count, count - steps))
    return lax.ppermute(value, axis, [(source, source + steps) for source in range(initial, last)])


def layer_norm(value, gain, shift):
    centre = jnp.mean(value, axis=-1, keepdims=True)
    centred = value - centre
    spread = jnp.mean(centred * centred, axis=-1, keepdims=True)
    return centred * lax.rsqrt(spread + EPSILON) * gain + shift


def positions(length, width):
    steps = jnp.arange(length, dtype=jnp.float32)
    bands = jnp.arange(1, 17, dtype=jnp.float32)
    angles = 2.0 * jnp.pi * steps[:, None] * bands[None, :] / length
    table = jnp.concatenate([(steps / length)[:, None], jnp.cos(angles), jnp.sin(angles)], axis=1)
    rates = jnp.exp(jnp.linspace(math.log(0.3), math.log(30.0), width)).astype(jnp.float32)
    decay = jnp.exp(-(steps / length)[:, None] * rates[None, :])
    return (table, decay)


def precise(left, right):
    return jnp.matmul(left, right, precision=lax.Precision.HIGHEST)


def filter_taps(embed_weight, embed_bias, filter_weight, filter_bias, taps_weight, length):
    table, decay = positions(length, taps_weight.shape[-1])
    first = jnp.sin(precise(table, embed_weight) + embed_bias)
    second = jnp.sin(precise(first, filter_weight) + filter_bias)
    return precise(second, taps_weight) * decay


def segment_ids(lengths, length):
    ends = jnp.cumsum(lengths, axis=-1)
    steps = jnp.arange(length, dtype=jnp.int32)
    return jnp.sum((steps[..., :, None] >= ends[..., None, :]).astype(jnp.int32), axis=-1)


def shift_rows(value, offset):
    length = value.shape[-2]
    padded = jnp.concatenate([jnp.zeros_like(value), value], axis=-2)
    return lax.dynamic_slice_in_dim(padded, length - offset, length, axis=-2)


def shift_ids(segments, offset):
    length = segments.shape[-1]
    padded = jnp.concatenate([jnp.full_like(segments, -1), segments], axis=-1)
    return lax.dynamic_slice_in_dim(padded, length - offset, length, axis=-1)


def mixer(project, short_kernel, taps, skip_gain, segments):
    length = project.shape[-2]
    convolved = short_kernel[0] * project
    for offset in (1, 2):
        same_doc = (segments == shift_ids(segments, offset))[..., None]
        convolved = convolved + short_kernel[offset] * jnp.where(
            same_doc, shift_rows(project, offset), 0.0
        )
    width = project.shape[-1] // 3
    gate_out = convolved[..., :width]
    gate_in = convolved[..., width : 2 * width]
    values = convolved[..., 2 * width :]
    mixed = values * gate_in
    steps = jnp.arange(length, dtype=jnp.int32)
    lags = steps[:, None] - steps[None, :]
    usable = jnp.logical_and(lags >= 0, segments[:, None] == segments[None, :])
    toeplitz = jnp.where(usable[..., None], taps[jnp.clip(lags, 0, length - 1)], 0.0)
    longconv = skip_gain * mixed + jnp.einsum(
        "tsd,sd->td", toeplitz, mixed, precision=lax.Precision.HIGHEST
    )
    return longconv * gate_out


def layer_forward(stream, weights, taps, segments):
    (
        mixer_gain,
        mixer_shift,
        input_weight,
        input_bias,
        short_kernel,
        skip_gain,
        output_weight,
        output_bias,
        feed_gain,
        feed_shift,
        up_weight,
        up_bias,
        down_weight,
        down_bias,
    ) = weights
    normed = layer_norm(stream, mixer_gain, mixer_shift).astype(jnp.bfloat16)
    project = jnp.dot(normed, input_weight, preferred_element_type=jnp.float32) + input_bias
    gated = mixer(project, short_kernel, taps, skip_gain, segments).astype(jnp.bfloat16)
    middle = (
        stream + jnp.dot(gated, output_weight, preferred_element_type=jnp.float32) + output_bias
    )
    second = layer_norm(middle, feed_gain, feed_shift).astype(jnp.bfloat16)
    before = jnp.dot(second, up_weight, preferred_element_type=jnp.float32) + up_bias
    activated = jax.nn.gelu(before, approximate=False).astype(jnp.bfloat16)
    result = (
        middle + jnp.dot(activated, down_weight, preferred_element_type=jnp.float32) + down_bias
    )
    return (result, (stream, normed, project, gated, middle, second, before, activated))


def layer_backward(grad_out, cache, weights, taps, segments):
    (
        mixer_gain,
        mixer_shift,
        input_weight,
        input_bias,
        short_kernel,
        skip_gain,
        output_weight,
        output_bias,
        feed_gain,
        feed_shift,
        up_weight,
        up_bias,
        down_weight,
        down_bias,
    ) = weights
    stream, normed, project, gated, middle, second, before, activated = cache
    grad_down = grad_out.astype(jnp.bfloat16)
    grad_act = jnp.dot(grad_down, down_weight.T, preferred_element_type=jnp.float32)
    _, gelu_back = jax.vjp(lambda inside: jax.nn.gelu(inside, approximate=False), before)
    grad_before = gelu_back(grad_act)[0]
    grad_hidden = grad_before.astype(jnp.bfloat16)
    grad_second = jnp.dot(grad_hidden, up_weight.T, preferred_element_type=jnp.float32)
    _, feed_back = jax.vjp(layer_norm, middle, feed_gain, feed_shift)
    grad_middle, grad_feed_gain, grad_feed_shift = feed_back(grad_second)
    grad_middle = grad_middle + grad_out
    grad_mid_low = grad_middle.astype(jnp.bfloat16)
    grad_gated = jnp.dot(grad_mid_low, output_weight.T, preferred_element_type=jnp.float32)
    _, mixer_back = jax.vjp(
        lambda first, second_arg, third, fourth: mixer(first, second_arg, third, fourth, segments),
        project,
        short_kernel,
        taps,
        skip_gain,
    )
    grad_project, grad_short, grad_taps, grad_skip = mixer_back(grad_gated)
    grad_proj_low = grad_project.astype(jnp.bfloat16)
    grad_normed = jnp.dot(grad_proj_low, input_weight.T, preferred_element_type=jnp.float32)
    _, mixer_norm_back = jax.vjp(layer_norm, stream, mixer_gain, mixer_shift)
    grad_stream, grad_mixer_gain, grad_mixer_shift = mixer_norm_back(grad_normed)
    grad_stream = grad_stream + grad_middle
    records = (
        normed,
        grad_proj_low,
        gated,
        grad_mid_low,
        second,
        grad_hidden,
        activated,
        grad_down,
    )
    sums = (
        grad_mixer_gain,
        grad_mixer_shift,
        jnp.sum(grad_project, axis=0),
        grad_short,
        grad_taps,
        grad_skip,
        jnp.sum(grad_middle, axis=0),
        grad_feed_gain,
        grad_feed_shift,
        jnp.sum(grad_before, axis=0),
        jnp.sum(grad_out, axis=0),
    )
    return (grad_stream, records, sums)


def prepare(full, length):
    ready = tuple(
        (
            piece if position in MATRICES else piece.astype(jnp.float32)
            for position, piece in enumerate(full)
        )
    )
    layers = []
    for inner in range(2):
        take = tuple((piece[inner] for piece in ready))
        taps = filter_taps(take[5], take[6], take[7], take[8], take[9], length)
        weights = (
            take[0],
            take[1],
            take[2],
            take[3],
            take[4],
            take[10],
            take[11],
            take[12],
            take[13],
            take[14],
            take[15],
            take[16],
            take[17],
            take[18],
        )
        layers.append((weights, taps))
    return (ready, layers)


def section_forward(entering, layers, segments):
    stream = entering
    caches = []
    for weights, taps in layers:
        stream, cache = layer_forward(stream, weights, taps, segments)
        caches.append(cache)
    return (stream, tuple(caches))


def section_backward(gradient, caches, layers, segments):
    records = [None, None]
    sums = [None, None]
    for inner in (1, 0):
        weights, taps = layers[inner]
        gradient, records[inner], sums[inner] = layer_backward(
            gradient, caches[inner], weights, taps, segments
        )
    return (gradient, tuple(records), tuple(sums))


def record_buffers(micro, length, width, hidden_width):

    def single():
        return (
            jnp.zeros((micro, length, width), jnp.bfloat16),
            jnp.zeros((micro, length, 3 * width), jnp.bfloat16),
            jnp.zeros((micro, length, width), jnp.bfloat16),
            jnp.zeros((micro, length, width), jnp.bfloat16),
            jnp.zeros((micro, length, width), jnp.bfloat16),
            jnp.zeros((micro, length, hidden_width), jnp.bfloat16),
            jnp.zeros((micro, length, hidden_width), jnp.bfloat16),
            jnp.zeros((micro, length, width), jnp.bfloat16),
        )

    return (single(), single())


def sum_zeros(length, width, hidden_width):

    def single():
        return (
            jnp.zeros((width,), jnp.float32),
            jnp.zeros((width,), jnp.float32),
            jnp.zeros((3 * width,), jnp.float32),
            jnp.zeros((3, 3 * width), jnp.float32),
            jnp.zeros((length, width), jnp.float32),
            jnp.zeros((width,), jnp.float32),
            jnp.zeros((width,), jnp.float32),
            jnp.zeros((width,), jnp.float32),
            jnp.zeros((width,), jnp.float32),
            jnp.zeros((hidden_width,), jnp.float32),
            jnp.zeros((width,), jnp.float32),
        )

    return (single(), single())


def place(buffer, piece, micro_slot):
    return lax.dynamic_update_index_in_dim(buffer, piece, micro_slot, 0)


def contract(left, right):
    return jnp.einsum("mla,mlb->ab", left, right, preferred_element_type=jnp.float32)


def on_device(
    tokens,
    cotangent,
    lengths,
    mixer_gain,
    mixer_shift,
    input_weight,
    input_bias,
    short_kernel,
    embed_weight,
    embed_bias,
    filter_weight,
    filter_bias,
    taps_weight,
    skip_gain,
    output_weight,
    output_bias,
    feed_gain,
    feed_shift,
    up_weight,
    up_bias,
    down_weight,
    down_bias,
):
    gathered = (
        lax.all_gather(mixer_gain, "dp", axis=1, tiled=True),
        lax.all_gather(mixer_shift, "dp", axis=1, tiled=True),
        lax.all_gather(input_weight, "dp", axis=1, tiled=True),
        lax.all_gather(input_bias, "dp", axis=1, tiled=True),
        lax.all_gather(short_kernel, "dp", axis=2, tiled=True),
        lax.all_gather(embed_weight, "dp", axis=2, tiled=True),
        lax.all_gather(embed_bias, "dp", axis=1, tiled=True),
        lax.all_gather(filter_weight, "dp", axis=2, tiled=True),
        lax.all_gather(filter_bias, "dp", axis=1, tiled=True),
        lax.all_gather(taps_weight, "dp", axis=2, tiled=True),
        lax.all_gather(skip_gain, "dp", axis=1, tiled=True),
        lax.all_gather(output_weight, "dp", axis=1, tiled=True),
        lax.all_gather(output_bias, "dp", axis=1, tiled=True),
        lax.all_gather(feed_gain, "dp", axis=1, tiled=True),
        lax.all_gather(feed_shift, "dp", axis=1, tiled=True),
        lax.all_gather(up_weight, "dp", axis=1, tiled=True),
        lax.all_gather(up_bias, "dp", axis=1, tiled=True),
        lax.all_gather(down_weight, "dp", axis=1, tiled=True),
        lax.all_gather(down_bias, "dp", axis=1, tiled=True),
    )
    section_index = lax.axis_index("section")
    sections = lax.axis_size("section")
    micro, length, width = tokens.shape
    hidden_width = gathered[15].shape[-1]
    segments = segment_ids(lengths, length)
    ready, layers = prepare(gathered, length)
    steps_total = micro + sections - 1
    kept = ()

    def forward_turn(turn_index, carry):
        incoming, saved, produced, kept_now = carry
        current = turn_index - section_index
        active = jnp.logical_and(current >= 0, current < micro)
        micro_slot = jnp.clip(current, 0, micro - 1)

        def forward_work(buffers):
            saved_now, produced_now, kept_inner = buffers
            fresh_rows = lax.dynamic_index_in_dim(tokens, micro_slot, 0, keepdims=False).astype(
                jnp.float32
            )
            entering = jnp.where(section_index == 0, fresh_rows, incoming)
            row_ids = lax.dynamic_index_in_dim(segments, micro_slot, 0, keepdims=False)
            result, caches = section_forward(entering, layers, row_ids)
            saved_now = place(saved_now, entering, micro_slot)
            produced_now = place(produced_now, result, micro_slot)
            return (result, saved_now, produced_now, kept_inner)

        def forward_skip_turn(buffers):
            return (jnp.zeros_like(incoming),) + buffers

        outgoing, saved, produced, kept_now = lax.cond(
            active, forward_work, forward_skip_turn, (saved, produced, kept_now)
        )
        incoming = from_behind(outgoing, "section", 1)
        return (incoming, saved, produced, kept_now)

    start = (
        jnp.zeros((length, width), jnp.float32),
        jnp.zeros(tokens.shape, jnp.float32),
        jnp.zeros(tokens.shape, jnp.float32),
        kept,
    )
    _, saved, produced, kept = lax.fori_loop(0, steps_total, forward_turn, start)
    regathered = (
        lax.all_gather(mixer_gain, "dp", axis=1, tiled=True),
        lax.all_gather(mixer_shift, "dp", axis=1, tiled=True),
        lax.all_gather(input_weight, "dp", axis=1, tiled=True),
        lax.all_gather(input_bias, "dp", axis=1, tiled=True),
        lax.all_gather(short_kernel, "dp", axis=2, tiled=True),
        lax.all_gather(embed_weight, "dp", axis=2, tiled=True),
        lax.all_gather(embed_bias, "dp", axis=1, tiled=True),
        lax.all_gather(filter_weight, "dp", axis=2, tiled=True),
        lax.all_gather(filter_bias, "dp", axis=1, tiled=True),
        lax.all_gather(taps_weight, "dp", axis=2, tiled=True),
        lax.all_gather(skip_gain, "dp", axis=1, tiled=True),
        lax.all_gather(output_weight, "dp", axis=1, tiled=True),
        lax.all_gather(output_bias, "dp", axis=1, tiled=True),
        lax.all_gather(feed_gain, "dp", axis=1, tiled=True),
        lax.all_gather(feed_shift, "dp", axis=1, tiled=True),
        lax.all_gather(up_weight, "dp", axis=1, tiled=True),
        lax.all_gather(up_bias, "dp", axis=1, tiled=True),
        lax.all_gather(down_weight, "dp", axis=1, tiled=True),
        lax.all_gather(down_bias, "dp", axis=1, tiled=True),
    )
    ready, layers = prepare(regathered, length)

    def backward_turn(turn_index, carry):
        incoming, grads_in, records, sums = carry
        current = turn_index - (sections - 1 - section_index)
        active = jnp.logical_and(current >= 0, current < micro)
        micro_slot = jnp.clip(current, 0, micro - 1)

        def backward_work(buffers):
            grads_now, records_now, sums_now = buffers
            fresh_rows = lax.dynamic_index_in_dim(cotangent, micro_slot, 0, keepdims=False).astype(
                jnp.float32
            )
            entering = jnp.where(section_index == sections - 1, fresh_rows, incoming)
            row_ids = lax.dynamic_index_in_dim(segments, micro_slot, 0, keepdims=False)
            section_input = lax.dynamic_index_in_dim(saved, micro_slot, 0, keepdims=False)
            caches = section_forward(section_input, layers, row_ids)[1]
            grad_entry, new_records, new_sums = section_backward(entering, caches, layers, row_ids)
            grads_now = place(grads_now, grad_entry, micro_slot)
            records_now = jax.tree.map(
                lambda buffer, piece: place(buffer, piece, micro_slot), records_now, new_records
            )
            sums_now = jax.tree.map(lambda total, piece: total + piece, sums_now, new_sums)
            return (grad_entry, grads_now, records_now, sums_now)

        def backward_skip_turn(buffers):
            return (jnp.zeros_like(incoming),) + buffers

        outgoing, grads_in, records, sums = lax.cond(
            active, backward_work, backward_skip_turn, (grads_in, records, sums)
        )
        incoming = from_behind(outgoing, "section", -1)
        return (incoming, grads_in, records, sums)

    start = (
        jnp.zeros((length, width), jnp.float32),
        jnp.zeros(tokens.shape, jnp.float32),
        record_buffers(micro, length, width, hidden_width),
        sum_zeros(length, width, hidden_width),
    )
    _, grads_in, records, sums = lax.fori_loop(0, steps_total, backward_turn, start)

    def layer_grads(inner):
        normed, grad_proj_low, gated, grad_mid_low, second, grad_hidden, activated, grad_down = (
            records[inner]
        )
        _, filter_back = jax.vjp(
            lambda first, second_arg, third, fourth, fifth: filter_taps(
                first, second_arg, third, fourth, fifth, length
            ),
            ready[5][inner],
            ready[6][inner],
            ready[7][inner],
            ready[8][inner],
            ready[9][inner],
        )
        filters = filter_back(sums[inner][4])
        part = sums[inner]
        return (
            part[0],
            part[1],
            contract(normed, grad_proj_low),
            part[2],
            part[3],
            filters[0],
            filters[1],
            filters[2],
            filters[3],
            filters[4],
            part[5],
            contract(gated, grad_mid_low),
            part[6],
            part[7],
            part[8],
            contract(second, grad_hidden),
            part[9],
            contract(activated, grad_down),
            part[10],
        )

    lower = layer_grads(0)
    upper = layer_grads(1)
    full_grads = tuple((jnp.stack([below, above]) for below, above in zip(lower, upper)))
    reduced = (
        lax.psum_scatter(full_grads[0], "dp", scatter_dimension=1, tiled=True),
        lax.psum_scatter(full_grads[1], "dp", scatter_dimension=1, tiled=True),
        lax.psum_scatter(full_grads[2], "dp", scatter_dimension=1, tiled=True),
        lax.psum_scatter(full_grads[3], "dp", scatter_dimension=1, tiled=True),
        lax.psum_scatter(full_grads[4], "dp", scatter_dimension=2, tiled=True),
        lax.psum_scatter(full_grads[5], "dp", scatter_dimension=2, tiled=True),
        lax.psum_scatter(full_grads[6], "dp", scatter_dimension=1, tiled=True),
        lax.psum_scatter(full_grads[7], "dp", scatter_dimension=2, tiled=True),
        lax.psum_scatter(full_grads[8], "dp", scatter_dimension=1, tiled=True),
        lax.psum_scatter(full_grads[9], "dp", scatter_dimension=2, tiled=True),
        lax.psum_scatter(full_grads[10], "dp", scatter_dimension=1, tiled=True),
        lax.psum_scatter(full_grads[11], "dp", scatter_dimension=1, tiled=True),
        lax.psum_scatter(full_grads[12], "dp", scatter_dimension=1, tiled=True),
        lax.psum_scatter(full_grads[13], "dp", scatter_dimension=1, tiled=True),
        lax.psum_scatter(full_grads[14], "dp", scatter_dimension=1, tiled=True),
        lax.psum_scatter(full_grads[15], "dp", scatter_dimension=1, tiled=True),
        lax.psum_scatter(full_grads[16], "dp", scatter_dimension=1, tiled=True),
        lax.psum_scatter(full_grads[17], "dp", scatter_dimension=1, tiled=True),
        lax.psum_scatter(full_grads[18], "dp", scatter_dimension=1, tiled=True),
    )
    return (produced[None], grads_in[None]) + tuple(reduced)


def solution(mesh):
    in_specs = (
        P("dp", None, None),
        P("dp", None, None),
        P("dp", None),
        P("section", "dp"),
        P("section", "dp"),
        P("section", "dp", None),
        P("section", "dp"),
        P("section", None, "dp"),
        P("section", None, "dp"),
        P("section", "dp"),
        P("section", None, "dp"),
        P("section", "dp"),
        P("section", None, "dp"),
        P("section", "dp"),
        P("section", "dp", None),
        P("section", "dp"),
        P("section", "dp"),
        P("section", "dp"),
        P("section", "dp", None),
        P("section", "dp"),
        P("section", "dp", None),
        P("section", "dp"),
    )
    out_specs = (
        P("section", "dp", None, None),
        P("section", "dp", None, None),
        P("section", "dp"),
        P("section", "dp"),
        P("section", "dp", None),
        P("section", "dp"),
        P("section", None, "dp"),
        P("section", None, "dp"),
        P("section", "dp"),
        P("section", None, "dp"),
        P("section", "dp"),
        P("section", None, "dp"),
        P("section", "dp"),
        P("section", "dp", None),
        P("section", "dp"),
        P("section", "dp"),
        P("section", "dp"),
        P("section", "dp", None),
        P("section", "dp"),
        P("section", "dp", None),
        P("section", "dp"),
    )
    return jax.shard_map(
        on_device, mesh=mesh, in_specs=in_specs, out_specs=out_specs, check_vma=False
    )
```

profile of v0, /device:TPU:25, one launch (start us, length us, event | category | flops | bytes accessed | tf_op | source)
XLA Modules:
  0.0 5266.8 jit_solution(12136032092962337658)
XLA Ops:
  153.8 23.5 all_gather.86
  192.7 120.8 %all-gather.7.cloned.1.call-done = bf16[2,1024,3072]{2,1,0:T(8,128)(2,1)} async-done(((bf16[2,256,3072]{2,1,0:T(8,128)(2,1)}), bf16[2,1024,3072]{2,1,0:T(8,128)(2,1)}) %all-gather.7.cloned.1.call-update) | async-done | bytes 12582928 | tf_op jit(solution)/shard_map/all_gather | solution.py:310
  324.0 276.0 %all-gather.11.cloned.1.call-done = bf16[2,1024,4096]{2,1,0:T(8,128)(2,1)} async-done(((bf16[2,256,4096]{2,1,0:T(8,128)(2,1)}), bf16[2,1024,4096]{2,1,0:T(8,128)(2,1)}) %all-gather.11.cloned.1.call-update) | async-done | bytes 16777232 | tf_op jit(solution)/shard_map/all_gather | solution.py:323
  612.5 273.9 %all-gather.13.cloned.1.call-done = bf16[2,4096,1024]{2,1,0:T(8,128)(2,1)} async-done(((bf16[2,1024,1024]{2,1,0:T(8,128)(2,1)}), bf16[2,4096,1024]{2,1,0:T(8,128)(2,1)}) %all-gather.13.cloned.1.call-update) | async-done | bytes 16777232 | tf_op jit(solution)/shard_map/all_gather | solution.py:325
  899.9 505.3 %while.109 = (s32[]{:T(128)}, f32[32,1024]{1,0:T(8,128)S(1)}, f32[4,32,1024]{2,1,0:T(8,128)}, f32[4,32,1024]{2,1,0:T(8,128)}, s32[]{:T(128)}, /*index=5*/bf16[4,...) while((s32[]{:T(128)}, f32[32,1024]{1,0:T(8,128)S(1)}, ...), condition=%wide.region_13.15_spmd, body=%wide.region_2.14_spmd.sunk | while | flops 1637624064 | bytes 83801824 | solution.py:370
  904.1 54.6 %collective-permute-done = f32[32,1024]{1,0:T(8,128)S(1)} collective-permute-done((f32[32,1024]{1,0:T(8,128)S(1)}, f32[32,1024]{1,0:T(8,128)S(1)}, u32[]{:S(2)}, u32[]{:S(2)}) %collective-permute-start) | collective-permute-done | bytes 131104 | tf_op jit(solution)/shard_map/while/body/eval_jaxpr/ppermute | solution.py:15
  958.8 55.8 %conditional.4 = (f32[32,1024]{1,0:T(8,128)S(1)}, f32[4,32,1024]{2,1,0:T(8,128)}, f32[4,32,1024]{2,1,0:T(8,128)}) conditional(s32[]{:T(128)} %convert_element_type.314, (f32[4,32,1024]{2,1,0:T(8,128)}, f32[4,32,1024]{2,1,0:T(8,128)}) %tuple.201, (s32[]{:T(128)}, s32[]{:T(128)}, bf16[4,32,1024]{2,1,0:T(8,128)(2,1)}, f32[32,1024]{1,0:T(8,128)S(1)}, ...), branch_computations={%region_3.4_spmd, %region_4.13_spmd} | conditional | flops 1637624064 | bytes 83276808 | solution.py:358
  1018.4 55.8 %conditional.4 = (f32[32,1024]{1,0:T(8,128)S(1)}, f32[4,32,1024]{2,1,0:T(8,128)}, f32[4,32,1024]{2,1,0:T(8,128)}) conditional(s32[]{:T(128)} %convert_element_type.314, (f32[4,32,1024]{2,1,0:T(8,128)}, f32[4,32,1024]{2,1,0:T(8,128)}) %tuple.201, (s32[]{:T(128)}, s32[]{:T(128)}, bf16[4,32,1024]{2,1,0:T(8,128)(2,1)}, f32[32,1024]{1,0:T(8,128)S(1)}, ...), branch_computations={%region_3.4_spmd, %region_4.13_spmd} | conditional | flops 1637624064 | bytes 83276808 | solution.py:358
  1080.4 55.7 %conditional.4 = (f32[32,1024]{1,0:T(8,128)S(1)}, f32[4,32,1024]{2,1,0:T(8,128)}, f32[4,32,1024]{2,1,0:T(8,128)}) conditional(s32[]{:T(128)} %convert_element_type.314, (f32[4,32,1024]{2,1,0:T(8,128)}, f32[4,32,1024]{2,1,0:T(8,128)}) %tuple.201, (s32[]{:T(128)}, s32[]{:T(128)}, bf16[4,32,1024]{2,1,0:T(8,128)(2,1)}, f32[32,1024]{1,0:T(8,128)S(1)}, ...), branch_computations={%region_3.4_spmd, %region_4.13_spmd} | conditional | flops 1637624064 | bytes 83276808 | solution.py:358
  1142.5 55.8 %conditional.4 = (f32[32,1024]{1,0:T(8,128)S(1)}, f32[4,32,1024]{2,1,0:T(8,128)}, f32[4,32,1024]{2,1,0:T(8,128)}) conditional(s32[]{:T(128)} %convert_element_type.314, (f32[4,32,1024]{2,1,0:T(8,128)}, f32[4,32,1024]{2,1,0:T(8,128)}) %tuple.201, (s32[]{:T(128)}, s32[]{:T(128)}, bf16[4,32,1024]{2,1,0:T(8,128)(2,1)}, f32[32,1024]{1,0:T(8,128)S(1)}, ...), branch_computations={%region_3.4_spmd, %region_4.13_spmd} | conditional | flops 1637624064 | bytes 83276808 | solution.py:358
  1204.5 60.1 %collective-permute-start = (f32[32,1024]{1,0:T(8,128)S(1)}, f32[32,1024]{1,0:T(8,128)S(1)}, u32[]{:S(2)}, u32[]{:S(2)}) collective-permute-start(f32[32,1024]{1,0:T(8,128)S(1)} %get-tuple-element.4111), channel_id=1, source_target_pairs={{0,4},{4,8},{8,12},{12,16},{16,20},{20,24},{24,28},{1,5},{5,9},{9,... | collective-permute-start | bytes 393224 | tf_op jit(solution)/shard_map/while/body/eval_jaxpr/ppermute | solution.py:15
  1272.9 53.6 %collective-permute-start = (f32[32,1024]{1,0:T(8,128)S(1)}, f32[32,1024]{1,0:T(8,128)S(1)}, u32[]{:S(2)}, u32[]{:S(2)}) collective-permute-start(f32[32,1024]{1,0:T(8,128)S(1)} %get-tuple-element.4111), channel_id=1, source_target_pairs={{0,4},{4,8},{8,12},{12,16},{16,20},{20,24},{24,28},{1,5},{5,9},{9,... | collective-permute-start | bytes 393224 | tf_op jit(solution)/shard_map/while/body/eval_jaxpr/ppermute | solution.py:15
  1335.1 61.0 %collective-permute-start = (f32[32,1024]{1,0:T(8,128)S(1)}, f32[32,1024]{1,0:T(8,128)S(1)}, u32[]{:S(2)}, u32[]{:S(2)}) collective-permute-start(f32[32,1024]{1,0:T(8,128)S(1)} %get-tuple-element.4111), channel_id=1, source_target_pairs={{0,4},{4,8},{8,12},{12,16},{16,20},{20,24},{24,28},{1,5},{5,9},{9,... | collective-permute-start | bytes 393224 | tf_op jit(solution)/shard_map/while/body/eval_jaxpr/ppermute | solution.py:15
  1433.0 1810.4 %while.110 = (s32[]{:T(128)}, f32[32,1024]{1,0:T(8,128)}, f32[4,32,1024]{2,1,0:T(8,128)}, bf16[4,32,1024]{2,1,0:T(8,128)(2,1)}, bf16[4,32,3072]{2,1,0:T(8,128)(2...) while((s32[]{:T(128)}, f32[32,1024]{1,0:T(8,128)}, ...), condition=%wide.region_59.61_spmd, body=%wide.region_14.60_spmd.sunk | while | flops 3020078336 | bytes 383339392 | solution.py:432
  1442.2 53.7 %collective-permute-done.1 = f32[32,1024]{1,0:T(8,128)S(1)} collective-permute-done((f32[32,1024]{1,0:T(8,128)}, f32[32,1024]{1,0:T(8,128)S(1)}, u32[]{:S(2)}, u32[]{:S(2)}) %collective-permute-start.1) | collective-permute-done | bytes 131104 | tf_op jit(solution)/shard_map/while/body/eval_jaxpr/ppermute | solution.py:15
  1507.6 57.7 %collective-permute-done.1 = f32[32,1024]{1,0:T(8,128)S(1)} collective-permute-done((f32[32,1024]{1,0:T(8,128)}, f32[32,1024]{1,0:T(8,128)S(1)}, u32[]{:S(2)}, u32[]{:S(2)}) %collective-permute-start.1) | collective-permute-done | bytes 131104 | tf_op jit(solution)/shard_map/while/body/eval_jaxpr/ppermute | solution.py:15
  1577.2 53.5 %collective-permute-done.1 = f32[32,1024]{1,0:T(8,128)S(1)} collective-permute-done((f32[32,1024]{1,0:T(8,128)}, f32[32,1024]{1,0:T(8,128)S(1)}, u32[]{:S(2)}, u32[]{:S(2)}) %collective-permute-start.1) | collective-permute-done | bytes 131104 | tf_op jit(solution)/shard_map/while/body/eval_jaxpr/ppermute | solution.py:15
  1634.0 848.1 %collective-permute-done.1 = f32[32,1024]{1,0:T(8,128)S(1)} collective-permute-done((f32[32,1024]{1,0:T(8,128)}, f32[32,1024]{1,0:T(8,128)S(1)}, u32[]{:S(2)}, u32[]{:S(2)}) %collective-permute-start.1) | collective-permute-done | bytes 131104 | tf_op jit(solution)/shard_map/while/body/eval_jaxpr/ppermute | solution.py:15
  2482.7 142.8 %conditional.5 = (f32[32,1024]{1,0:T(8,128)}, f32[4,32,1024]{2,1,0:T(8,128)}, bf16[4,32,1024]{2,1,0:T(8,128)(2,1)}, bf16[4,32,3072]{2,1,0:T(8,128)(2,1)}, bf16[4...) conditional(s32[]{:T(128)} %convert_element_type.315, ...), branch_computations={%region_15.16_spmd, %region_16.59_spmd} | conditional | flops 3020078336 | bytes 382289152 | solution.py:420
  2638.3 143.5 %conditional.5 = (f32[32,1024]{1,0:T(8,128)}, f32[4,32,1024]{2,1,0:T(8,128)}, bf16[4,32,1024]{2,1,0:T(8,128)(2,1)}, bf16[4,32,3072]{2,1,0:T(8,128)(2,1)}, bf16[4...) conditional(s32[]{:T(128)} %convert_element_type.315, ...), branch_computations={%region_15.16_spmd, %region_16.59_spmd} | conditional | flops 3020078336 | bytes 382289152 | solution.py:420
  2790.6 143.4 %conditional.5 = (f32[32,1024]{1,0:T(8,128)}, f32[4,32,1024]{2,1,0:T(8,128)}, bf16[4,32,1024]{2,1,0:T(8,128)(2,1)}, bf16[4,32,3072]{2,1,0:T(8,128)(2,1)}, bf16[4...) conditional(s32[]{:T(128)} %convert_element_type.315, ...), branch_computations={%region_15.16_spmd, %region_16.59_spmd} | conditional | flops 3020078336 | bytes 382289152 | solution.py:420
  2941.3 143.2 %conditional.5 = (f32[32,1024]{1,0:T(8,128)}, f32[4,32,1024]{2,1,0:T(8,128)}, bf16[4,32,1024]{2,1,0:T(8,128)(2,1)}, bf16[4,32,3072]{2,1,0:T(8,128)(2,1)}, bf16[4...) conditional(s32[]{:T(128)} %convert_element_type.315, ...), branch_computations={%region_15.16_spmd, %region_16.59_spmd} | conditional | flops 3020078336 | bytes 382289152 | solution.py:420
  3098.2 135.9 %collective-permute-start.1 = (f32[32,1024]{1,0:T(8,128)}, f32[32,1024]{1,0:T(8,128)S(1)}, u32[]{:S(2)}, u32[]{:S(2)}) collective-permute-start(f32[32,1024]{1,0:T(8,128)} %get-tuple-element.4189), channel_id=1, source_target_pairs={{4,0},{8,4},{12,8},{16,12},{20,16},{24,20},{28,24},{5,1},{9,5},{13... | collective-permute-start | bytes 393224 | tf_op jit(solution)/shard_map/while/body/eval_jaxpr/ppermute | solution.py:15
  3396.2 20.5 reduce-scatter.54.cloned.1.call-done
  3418.3 20.7 reduce-scatter.52.cloned.1.call-done
  3440.6 35.8 reduce-scatter.56.cloned.1.call-done
  3478.1 43.6 reduce-scatter.72.cloned.1.call-done
  3523.6 34.7 reduce-scatter.58.cloned.1.call-done
  3580.2 148.8 %reduce-scatter.46.cloned.1.call-done = f32[2,256,1024]{2,1,0:T(8,128)} async-done(((f32[2,1024,1024]{2,1,0:T(8,128)}), f32[2,256,1024]{2,1,0:T(8,128)}) %reduce-scatter.46.cloned.1.call-update) | async-done | bytes 2097168 | tf_op jit(solution)/shard_map/reduce_scatter | solution.py:487
  3729.0 419.3 %reduce-scatter.42.cloned.1.call-done = f32[2,256,3072]{2,1,0:T(8,128)} async-done(((f32[2,1024,3072]{2,1,0:T(8,128)}), f32[2,256,3072]{2,1,0:T(8,128)}) %reduce-scatter.42.cloned.1.call-update) | async-done | bytes 6291472 | tf_op jit(solution)/shard_map/reduce_scatter | solution.py:478
  4148.3 555.6 %reduce-scatter.50.cloned.1.call-done = f32[2,1024,1024]{2,1,0:T(8,128)} async-done(((f32[2,4096,1024]{2,1,0:T(8,128)}), f32[2,1024,1024]{2,1,0:T(8,128)}) %reduce-scatter.50.cloned.1.call-update) | async-done | bytes 8388624 | tf_op jit(solution)/shard_map/reduce_scatter | solution.py:493
  4703.9 555.9 %reduce-scatter.48.cloned.1.call-done = f32[2,256,4096]{2,1,0:T(8,128)} async-done(((f32[2,1024,4096]{2,1,0:T(8,128)}), f32[2,256,4096]{2,1,0:T(8,128)}) %reduce-scatter.48.cloned.1.call-update) | async-done | bytes 8388624 | tf_op jit(solution)/shard_map/reduce_scatter | solution.py:491
  (1885 shorter events, 1329.9 us)
Async XLA Ops:
  7.4 181.3 %all-gather.9.cloned.1.call-start = ((), (), s32[]{:S(2)}) async-start(), calls=%async_computation.18 | async-start | bytes 5242880 | tf_op jit(solution)/shard_map/all_gather | solution.py:319
  8.1 305.4 %all-gather.7.cloned.1.call-start = ((), (), s32[]{:S(2)}) async-start(), calls=%async_computation.17 | async-start | bytes 15728640 | tf_op jit(solution)/shard_map/all_gather | solution.py:310
  8.8 591.2 %all-gather.11.cloned.1.call-start = ((), (), s32[]{:S(2)}) async-start(), calls=%async_computation.19 | async-start | bytes 20971520 | tf_op jit(solution)/shard_map/all_gather | solution.py:323
  9.6 876.9 %all-gather.13.cloned.1.call-start = ((), (), s32[]{:S(2)}) async-start(), calls=%async_computation.20 | async-start | bytes 20971520 | tf_op jit(solution)/shard_map/all_gather | solution.py:325
  10.2 3350.4 %reduce-scatter.62.cloned.1.call-start = ((), (), s32[]{:S(2)}) async-start(), calls=%async_computation.31 | async-start | bytes 40960
  900.4 58.3 %collective-permute-start = (f32[32,1024]{1,0:T(8,128)S(1)}, f32[32,1024]{1,0:T(8,128)S(1)}, u32[]{:S(2)}, u32[]{:S(2)}) collective-permute-start(f32[32,1024]{1,0:T(8,128)S(1)} %get-tuple-element.4111), channel_id=1, source_target_pairs={{0,4},{4,8},{8,12},{12,16},{16,20},{20,24},{24,28},{1,5},{5,9},{9,... | collective-permute-start | bytes 393224 | tf_op jit(solution)/shard_map/while/body/eval_jaxpr/ppermute | solution.py:15
  1204.5 62.0 %collective-permute-start = (f32[32,1024]{1,0:T(8,128)S(1)}, f32[32,1024]{1,0:T(8,128)S(1)}, u32[]{:S(2)}, u32[]{:S(2)}) collective-permute-start(f32[32,1024]{1,0:T(8,128)S(1)} %get-tuple-element.4111), channel_id=1, source_target_pairs={{0,4},{4,8},{8,12},{12,16},{16,20},{20,24},{24,28},{1,5},{5,9},{9,... | collective-permute-start | bytes 393224 | tf_op jit(solution)/shard_map/while/body/eval_jaxpr/ppermute | solution.py:15
  1272.9 55.6 %collective-permute-start = (f32[32,1024]{1,0:T(8,128)S(1)}, f32[32,1024]{1,0:T(8,128)S(1)}, u32[]{:S(2)}, u32[]{:S(2)}) collective-permute-start(f32[32,1024]{1,0:T(8,128)S(1)} %get-tuple-element.4111), channel_id=1, source_target_pairs={{0,4},{4,8},{8,12},{12,16},{16,20},{20,24},{24,28},{1,5},{5,9},{9,... | collective-permute-start | bytes 393224 | tf_op jit(solution)/shard_map/while/body/eval_jaxpr/ppermute | solution.py:15
  1335.1 62.9 %collective-permute-start = (f32[32,1024]{1,0:T(8,128)S(1)}, f32[32,1024]{1,0:T(8,128)S(1)}, u32[]{:S(2)}, u32[]{:S(2)}) collective-permute-start(f32[32,1024]{1,0:T(8,128)S(1)} %get-tuple-element.4111), channel_id=1, source_target_pairs={{0,4},{4,8},{8,12},{12,16},{16,20},{20,24},{24,28},{1,5},{5,9},{9,... | collective-permute-start | bytes 393224 | tf_op jit(solution)/shard_map/while/body/eval_jaxpr/ppermute | solution.py:15
  1440.3 55.6 %collective-permute-start.1 = (f32[32,1024]{1,0:T(8,128)}, f32[32,1024]{1,0:T(8,128)S(1)}, u32[]{:S(2)}, u32[]{:S(2)}) collective-permute-start(f32[32,1024]{1,0:T(8,128)} %get-tuple-element.4189), channel_id=1, source_target_pairs={{4,0},{8,4},{12,8},{16,12},{20,16},{24,20},{28,24},{5,1},{9,5},{13... | collective-permute-start | bytes 393224 | tf_op jit(solution)/shard_map/while/body/eval_jaxpr/ppermute | solution.py:15
  1505.7 59.6 %collective-permute-start.1 = (f32[32,1024]{1,0:T(8,128)}, f32[32,1024]{1,0:T(8,128)S(1)}, u32[]{:S(2)}, u32[]{:S(2)}) collective-permute-start(f32[32,1024]{1,0:T(8,128)} %get-tuple-element.4189), channel_id=1, source_target_pairs={{4,0},{8,4},{12,8},{16,12},{20,16},{24,20},{28,24},{5,1},{9,5},{13... | collective-permute-start | bytes 393224 | tf_op jit(solution)/shard_map/while/body/eval_jaxpr/ppermute | solution.py:15
  1575.3 55.4 %collective-permute-start.1 = (f32[32,1024]{1,0:T(8,128)}, f32[32,1024]{1,0:T(8,128)S(1)}, u32[]{:S(2)}, u32[]{:S(2)}) collective-permute-start(f32[32,1024]{1,0:T(8,128)} %get-tuple-element.4189), channel_id=1, source_target_pairs={{4,0},{8,4},{12,8},{16,12},{20,16},{24,20},{28,24},{5,1},{9,5},{13... | collective-permute-start | bytes 393224 | tf_op jit(solution)/shard_map/while/body/eval_jaxpr/ppermute | solution.py:15
  1632.1 850.0 %collective-permute-start.1 = (f32[32,1024]{1,0:T(8,128)}, f32[32,1024]{1,0:T(8,128)S(1)}, u32[]{:S(2)}, u32[]{:S(2)}) collective-permute-start(f32[32,1024]{1,0:T(8,128)} %get-tuple-element.4189), channel_id=1, source_target_pairs={{4,0},{8,4},{12,8},{16,12},{20,16},{24,20},{28,24},{5,1},{9,5},{13... | collective-permute-start | bytes 393224 | tf_op jit(solution)/shard_map/while/body/eval_jaxpr/ppermute | solution.py:15
  2625.6 11.8 collective-permute-start.1
  2781.9 7.6 collective-permute-start.1
  3098.2 137.1 %collective-permute-start.1 = (f32[32,1024]{1,0:T(8,128)}, f32[32,1024]{1,0:T(8,128)S(1)}, u32[]{:S(2)}, u32[]{:S(2)}) collective-permute-start(f32[32,1024]{1,0:T(8,128)} %get-tuple-element.4189), channel_id=1, source_target_pairs={{4,0},{8,4},{12,8},{16,12},{20,16},{24,20},{28,24},{5,1},{9,5},{13... | collective-permute-start | bytes 393224 | tf_op jit(solution)/shard_map/while/body/eval_jaxpr/ppermute | solution.py:15
  3246.7 115.1 %reduce-scatter.60.cloned.1.call-start = ((), (), s32[]{:S(2)}) async-start(), calls=%async_computation.30 | async-start | bytes 40960
  3251.2 111.9 %reduce-scatter.66.cloned.1.call-start = ((), (), s32[]{:S(2)}) async-start(), calls=%async_computation.33 | async-start | bytes 655360
  3253.1 111.7 %reduce-scatter.68.cloned.1.call-start = ((), (), s32[]{:S(2)}) async-start(), calls=%async_computation.34 | async-start | bytes 655360
  3254.9 111.4 %reduce-scatter.70.cloned.1.call-start = ((), (), s32[]{:S(2)}) async-start(), calls=%async_computation.35 | async-start | bytes 655360
  3256.7 115.9 %reduce-scatter.74.cloned.1.call-start = ((), (), s32[]{:S(2)}) async-start(), calls=%async_computation.37 | async-start | bytes 655360
  3258.5 136.2 %reduce-scatter.64.cloned.1.call-start = ((), (), s32[]{:S(2)}) async-start(), calls=%async_computation.32 | async-start | bytes 655360
  3260.3 156.5 %reduce-scatter.54.cloned.1.call-start = ((), (), s32[]{:S(2)}) async-start(), calls=%async_computation.27 | async-start | bytes 655360
  3262.1 176.9 %reduce-scatter.52.cloned.1.call-start = ((), (), s32[]{:S(2)}) async-start(), calls=%async_computation.26 | async-start | bytes 655360
  3264.0 212.4 %reduce-scatter.56.cloned.1.call-start = ((), (), s32[]{:S(2)}) async-start(), calls=%async_computation.28 | async-start | bytes 1966080
  3266.5 255.2 %reduce-scatter.72.cloned.1.call-start = ((), (), s32[]{:S(2)}) async-start(), calls=%async_computation.36 | async-start | bytes 2621440
  3275.0 283.3 %reduce-scatter.58.cloned.1.call-start = ((), (), s32[]{:S(2)}) async-start(), calls=%async_computation.29 | async-start | bytes 1966080
  3275.6 304.6 %reduce-scatter.44.cloned.1.call-start = ((), (), s32[]{:S(2)}) async-start(), calls=%async_computation.22 | async-start | bytes 655360 | tf_op jit(solution)/shard_map/reduce_scatter | solution.py:485
  3276.9 452.1 %reduce-scatter.46.cloned.1.call-start = ((), (), s32[]{:S(2)}) async-start(), calls=%async_computation.23 | async-start | bytes 10485760 | tf_op jit(solution)/shard_map/reduce_scatter | solution.py:487
  3284.7 863.6 %reduce-scatter.42.cloned.1.call-start = ((), (), s32[]{:S(2)}) async-start(), calls=%async_computation.21 | async-start | bytes 31457280 | tf_op jit(solution)/shard_map/reduce_scatter | solution.py:478
  3299.6 1404.3 %reduce-scatter.50.cloned.1.call-start = ((), (), s32[]{:S(2)}) async-start(), calls=%async_computation.25 | async-start | bytes 41943040 | tf_op jit(solution)/shard_map/reduce_scatter | solution.py:493
  3320.0 1939.8 %reduce-scatter.48.cloned.1.call-start = ((), (), s32[]{:S(2)}) async-start(), calls=%async_computation.24 | async-start | bytes 41943040 | tf_op jit(solution)/shard_map/reduce_scatter | solution.py:491
  (534 other events, 5375.0 us)
Sparse Core Ops, SparseCore 0:
  9.8 80.2 all-gather.8
  91.6 221.8 all-gather.6
  315.1 284.9 all-gather.10
  601.5 284.9 all-gather.12
  3246.8 16.6 reduce-scatter.61
  3265.8 17.0 reduce-scatter.59
  3285.1 20.6 reduce-scatter.65
  3308.1 19.8 reduce-scatter.67
  3330.3 20.1 reduce-scatter.69
  3352.7 19.8 reduce-scatter.73
  3374.9 19.7 reduce-scatter.63
  3396.8 19.9 reduce-scatter.53
  3419.1 19.9 reduce-scatter.51
  3441.2 35.1 reduce-scatter.55
  3478.5 43.1 reduce-scatter.71
  3524.0 34.2 reduce-scatter.57
  3561.1 19.0 reduce-scatter.43
  3583.1 145.8 reduce-scatter.45
  3732.1 416.1 reduce-scatter.41
  4151.1 552.7 reduce-scatter.49
  4707.0 552.7 reduce-scatter.47
where the time goes:
time: 5280 us; the launch traced here: 5270 us
  waiting for transfers between devices  3680 us (70%)
  matrix products  401 us (8%)
  starting transfers between devices  364 us (7%)
  other arithmetic  336 us (6%)
  local copies, waits for them, and re-layouts  259 us (5%)
  blocking collectives  183 us (3%)
    ppermute x22, waiting for transfers between devices, from_behind(): lax.ppermute(value, axis, [(source, source + steps) for source in range(i...  1120 us
    reduce_scatter x1, waiting for transfers between devices, on_device(): lax.psum_scatter(full_grads[15], 'dp', scatter_dimension=1, tiled=True)  556 us
    reduce_scatter x1, waiting for transfers between devices, on_device(): lax.psum_scatter(full_grads[17], 'dp', scatter_dimension=1, tiled=True)  556 us
    reduce_scatter x1, waiting for transfers between devices, on_device(): lax.psum_scatter(full_grads[2], 'dp', scatter_dimension=1, tiled=True)  419 us
    ppermute x22, starting transfers between devices, from_behind(): lax.ppermute(value, axis, [(source, source + steps) for source in range(i...  363 us
    all_gather x1, waiting for transfers between devices, on_device(): lax.all_gather(up_weight, 'dp', axis=1, tiled=True)  276 us
    all_gather x1, waiting for transfers between devices, on_device(): lax.all_gather(down_weight, 'dp', axis=1, tiled=True)  274 us
    unnamed x33, waiting for transfers between devices  184 us
  transfers between devices with their start and end apart: 43, of which 37 were waited for; matrix products, arithmetic and copies ran while one was open for 3% of the time, Pallas kernels for 0%

commit v1 on v0

v1 whole, which is shorter than its diff:
```python
import functools
import math

import jax
import jax.numpy as jnp
import numpy as np
from jax import lax
from jax.experimental import pallas as pl
from jax.experimental.pallas import tpu as pltpu
from jax.sharding import PartitionSpec as P

EPSILON = 1e-05
MESH = pl.DeviceIdType.MESH
F32 = jnp.float32
BF16 = jnp.bfloat16
PLANES = 4
SMALL = 32
HIGH = lax.Precision.HIGHEST
HOPS = 4


def div(a, b):
    return lax.div(a, jnp.int32(b))


def rem(a, b):
    return lax.rem(a, jnp.int32(b))


def bits(count):
    return max(0, (count - 1).bit_length())


def gray(p, count):
    if count & (count - 1):
        return p
    return sum(
        (2**b * rem(rem(div(p, 2**b), 2) + rem(div(p, 2 ** (b + 1)), 2), 2) for b in range(bits(count))),
        jnp.int32(0),
    )


def ungray(c, count):
    if count & (count - 1):
        return c
    total = jnp.int32(0)
    for b in range(bits(count)):
        upper = sum((rem(div(c, 2**q), 2) for q in range(b, bits(count))), jnp.int32(0))
        total = total + 2**b * rem(upper, 2)
    return total


def snake(p, group, count):
    back = rem(group, 2)
    return p + back * (count - 1 - 2 * p)


def column_of(layer, columns):
    group = div(layer, columns)
    return gray(snake(rem(layer, columns), group, columns), columns)


def plane_of(layer, columns):
    return rem(div(layer, columns) + 1, PLANES)


def layer_of(column, plane, columns):
    group = rem(plane + PLANES - 1, PLANES)
    return group * columns + snake(ungray(column, columns), group, columns)


def fold(value):
    total = value[0:8]
    for step in range(8, value.shape[0], 8):
        total = total + value[step : step + 8]
    return total


def norm_parts(value):
    centred = value - jnp.mean(value, axis=-1, keepdims=True)
    rate = lax.rsqrt(jnp.mean(centred * centred, axis=-1, keepdims=True) + EPSILON)
    return centred * rate, rate


def norm_back(grad, gain, unit, rate):
    inner = grad * gain
    first = jnp.mean(inner, axis=-1, keepdims=True)
    second = jnp.mean(inner * unit, axis=-1, keepdims=True)
    return rate * (inner - first - unit * second)


def dot_right(left, right):
    return lax.dot_general(left, right, (((1,), (1,)), ((), ())), preferred_element_type=F32)


def dot_tokens(left, right, precision=None):
    return lax.dot_general(
        left, right, (((0,), (0,)), ((), ())), precision=precision, preferred_element_type=F32
    )


def kernel(
    size,
    tokens,
    cotangent,
    in_w,
    out_w,
    up_w,
    down_w,
    lengths,
    vectors,
    input_bias,
    short_kernel,
    up_bias,
    taps_weight,
    embed_weight,
    embed_bias,
    filter_weight,
    filter_bias,
    decay,
    table,
    g_in_w,
    g_out_w,
    g_up_w,
    g_down_w,
    g_small,
    g_filt,
    r_out,
    r_grad,
    rel,
    rel_down,
    back,
    back_down,
    w,
    sm,
    ft,
    own_sm,
    own_ft,
    own_mask,
    square,
    v1,
    bi,
    ks,
    bu,
    tw,
    taps,
    fstate,
    bm,
    s_in,
    g_arr,
    s_out,
    g_out,
    xn,
    xg,
    x2,
    xa,
    proj,
    conv,
    lcs,
    gpr,
    mid,
    dp,
    dg,
    dh,
    pxn,
    pxg,
    px2,
    pxa,
    pdp,
    pdg,
    pdh,
    pdm,
    a1,
    abi,
    aks,
    abu,
    atp,
    sgrad,
    fgrad,
    ws,
    rr,
    ls,
    wr,
    fs,
    fr,
    ps,
    pr,
    ms,
    mr,
    ts,
    cs,
    hfs,
    hfr,
    hbs,
    hbr,
    sos,
    sor,
    sgs,
    sgr,
    xs,
    xr,
    ds,
    dr,
    gs,
    gr,
    br,
    bs,
    vs,
    vr,
    lag_sem,
):
    S, n, R, D, FF, m, MT, lags, units, length = size
    C = S // 2
    dn, fn, un = D // n, FF // n, units // n
    h, fh = dn // 2, fn // 2
    wide = FF // D
    blocks = 4 + wide
    pieces = blocks + 1
    layers = PLANES * C
    s, z = lax.axis_index("section"), lax.axis_index("dp")
    k, c = rem(s, 2), div(s, 2)
    rho, plane = div(z, PLANES), rem(z, PLANES)
    other = s + 1 - 2 * k
    layer = layer_of(c, plane, C)
    own_s, own_e = div(layer, 2), rem(layer, 2)
    first, last = layer == 0, layer == layers - 1

    def chip_of(stage):
        return 2 * column_of(stage, C) + k, PLANES * rho + plane_of(stage, C)

    next_s, next_z = chip_of(jnp.minimum(layer + 1, layers - 1))
    prev_s, prev_z = chip_of(jnp.maximum(layer - 1, 0))

    def remote(src, dst, send, recv, to_s, to_z):
        return pltpu.make_async_remote_copy(
            src_ref=src,
            dst_ref=dst,
            send_sem=send,
            recv_sem=recv,
            device_id=(to_s, to_z),
            device_id_type=MESH,
        )

    def start(src, dst, send, recv, to_s, to_z, when=True):
        here = jnp.logical_and(to_s == s, to_z == z)

        @pl.when(jnp.logical_and(when, here))
        def _():
            pltpu.make_async_copy(src, dst, recv).start()

        @pl.when(jnp.logical_and(when, jnp.logical_not(here)))
        def _():
            remote(src, dst, send, recv, to_s, to_z).start()

    def sent(src, dst, send, recv, to_s, to_z, when=True):
        here = jnp.logical_and(to_s == s, to_z == z)

        @pl.when(jnp.logical_and(when, jnp.logical_not(here)))
        def _():
            remote(src, dst, send, recv, to_s, to_z).wait_send()

    def arrived(dst, recv):
        remote(dst, dst, recv, recv, other, z).wait_recv()

    def rows(index, count):
        return pl.ds(pl.multiple_of(index * count, count), count)

    barrier = pltpu.get_barrier_semaphore()

    @pl.loop(0, S)
    def _(a):
        @pl.loop(0, n)
        def _(b):
            @pl.when(jnp.logical_or(a != s, b != z))
            def _():
                pl.semaphore_signal(barrier, inc=1, device_id=(a, b), device_id_type=MESH)

    pl.semaphore_wait(barrier, S * n - 1)

    def relay_at(group, pos):
        return rel.at[group, pos] if pos < blocks else rel_down.at[group]

    def held_at(pos, q, core):
        if pos < blocks:
            return w.at[pos, rows(2 * q + core, h)]
        begin = q * fn + core * fh
        return w.at[blocks + div(begin, D), pl.ds(pl.multiple_of(rem(begin, D), fh), fh)]

    def source_at(e, core, pos):
        strip = pl.ds(core * h, h)
        if pos < 3:
            return in_w.at[e, strip, pl.ds(pos * D, D)]
        if pos == 3:
            return out_w.at[e, strip]
        if pos < blocks:
            return up_w.at[e, strip, pl.ds((pos - 4) * D, D)]
        return down_w.at[e, pl.ds(core * fh, fh)]

    def column_copies():
        for pos in range(pieces):
            for e in range(2):
                lay = 2 * s + e
                to_c, group = column_of(lay, C), div(lay, C)
                for core in range(2):
                    yield (
                        source_at(e, core, pos),
                        relay_at(group, pos),
                        ws.at[e, core, pos],
                        rr.at[group, pos],
                        2 * to_c + core,
                        z,
                    )

    def plane_copies(group, pos):
        to_p = (group + 1) % PLANES
        for copy in range(R):
            yield (
                relay_at(group, pos),
                held_at(pos, z, k),
                ls.at[group, copy, pos],
                wr.at[pos, z],
                s,
                PLANES * copy + to_p,
            )

    def pass_on(group, pos):
        arrived(relay_at(group, pos), rr.at[group, pos])
        for copy in plane_copies(group, pos):
            start(*copy)

    first_s, first_z = chip_of(jnp.int32(0))
    last_s, last_z = chip_of(jnp.int32(layers - 1))
    HW = D // HOPS

    def token_copies():
        at = rows(plane, MT)
        for part in range(HOPS):
            col = pl.ds(part * HW, HW)
            yield (
                tokens.at[rows(k, MT), col],
                s_in.at[at, col],
                ts.at[part],
                hfr.at[plane, part],
                first_s,
                first_z,
                s == first_s,
            )
        yield (
            cotangent.at[rows(k, MT)],
            g_arr.at[at],
            cs.at[0],
            hbr.at[plane],
            last_s,
            last_z,
            s == last_s,
        )

    def small_copies():
        for q in range(PLANES):
            yield (own_mask, bm.at[rows(plane, MT)], ms.at[q], mr.at[plane], s, PLANES * rho + q, True)
        for e in range(2):
            lay = 2 * s + e
            to_c, to_p = column_of(lay, C), plane_of(lay, C)
            for copy in range(R):
                to_z = PLANES * copy + to_p
                for core in range(2):
                    to = 2 * to_c + core
                    yield (own_sm.at[e], sm.at[z], ps.at[0, e, copy, core], pr.at[0, z], to, to_z)
                    yield (
                        own_ft.at[e],
                        ft.at[rows(z, un)],
                        ps.at[1, e, copy, core],
                        pr.at[1, z],
                        to,
                        to_z,
                    )

    for copy in token_copies():
        start(*copy)
    for copy in column_copies():
        start(*copy)

    step = lax.broadcasted_iota(jnp.int32, (length, 128), 0)
    for r in range(MT // length):
        begins = step == 0
        begin = jnp.int32(0)
        for doc in range(lengths.shape[1]):
            begin = begin + lengths[k * (MT // length) + r, doc]
            begins = jnp.logical_or(begins, step == begin)
        own_mask[r * length : (r + 1) * length, :] = jnp.where(begins, 0.0, 1.0)

    own_sm[...] = jnp.zeros_like(own_sm)
    for index in range(7):
        own_sm[:, index, :] = vectors[index, :, :].astype(F32)
    wide_bias, wide_up = input_bias[...].astype(F32), up_bias[...].astype(F32)
    for r in range(3):
        own_sm[:, 7 + r, :] = wide_bias[:, r * dn : (r + 1) * dn]
        for e in range(2):
            three = short_kernel[e].astype(F32)
            for tap in range(3):
                own_sm[e, 10 + 3 * tap + r, :] = three[tap, r * dn : (r + 1) * dn]
    for r in range(wide):
        own_sm[:, 19 + r, :] = wide_up[:, r * dn : (r + 1) * dn]
    own_sm[:, SMALL:, :] = taps_weight[...].astype(F32)
    for net, (weight, bias) in enumerate(((embed_weight, embed_bias), (filter_weight, filter_bias))):
        depth = weight.shape[1]
        for e in range(2):
            square[...] = jnp.zeros_like(square)
            square[0:depth, 0:un] = weight[e].astype(F32)
            square[depth : depth + 1, 0:un] = bias[e : e + 1, :].astype(F32)
            own_ft[e, :, net * 128 : (net + 1) * 128] = square[...].T[0:un, :]
    for copy in small_copies():
        start(*copy)

    ft[pl.ds(units, units), :] = jnp.zeros((units, 256), F32)
    a1[...] = jnp.zeros_like(a1)
    abi[...] = jnp.zeros_like(abi)
    aks[...] = jnp.zeros_like(aks)
    abu[...] = jnp.zeros_like(abu)
    atp[...] = jnp.zeros_like(atp)
    sgrad[...] = jnp.zeros_like(sgrad)

    for pos in range(pieces):
        for group in (0, 1):
            pass_on(group, pos)
        for near, group in ((1, 3), (2, 2)):

            @pl.when(plane == near)
            def _():
                pass_on(group, pos)

    defers = layer == C - 1

    def pass_rest():
        for pos in range(pieces):
            for near, group in ((1, 3), (2, 2)):

                @pl.when(plane != near)
                def _():
                    pass_on(group, pos)

    @pl.when(jnp.logical_not(defers))
    def _():
        pass_rest()

    @pl.loop(0, n)
    def _(q):
        arrived(sm.at[q], pr.at[0, q])
        arrived(ft.at[rows(q, un)], pr.at[1, q])

    for q in range(n):
        block = sm[q, 0:SMALL, :]
        v1[:, q * dn : (q + 1) * dn] = block[0:8]
        for r in range(3):
            at = slice((3 * q + r) * dn, (3 * q + r + 1) * dn)
            bi[0:1, at] = block[7 + r : 8 + r]
            for tap in range(3):
                ks[tap : tap + 1, at] = block[10 + 3 * tap + r : 11 + 3 * tap + r]
        for r in range(wide):
            at = slice((wide * q + r) * dn, (wide * q + r + 1) * dn)
            bu[0:1, at] = block[19 + r : 20 + r]
        tw[:, q * dn : (q + 1) * dn] = sm[q, SMALL : SMALL + units, :]

    lane = lax.broadcasted_iota(jnp.int32, (lags, 2 * units), 1)
    embed, deep = ft[:, 0:128], ft[:, 128:256]
    pre1 = lax.dot_general(
        table[...], embed, (((1,), (1,)), ((), ())), precision=HIGH, preferred_element_type=F32
    )
    one = jnp.where(lane == units, 1.0, jnp.sin(pre1))
    pre2 = lax.dot_general(
        one, deep, (((1,), (1,)), ((), ())), precision=HIGH, preferred_element_type=F32
    )
    two = jnp.sin(pre2)
    fstate[0] = one
    fstate[1] = jnp.cos(pre1)
    fstate[2] = two
    fstate[3] = jnp.cos(pre2)
    taps[...] = (
        jnp.dot(two[:, 0:units], tw[...], precision=HIGH, preferred_element_type=F32) * decay[...]
    )

    @pl.loop(0, PLANES)
    def _(q):
        arrived(bm.at[rows(q, MT)], mr.at[q])

    def share_copy(pos, q):
        at = held_at(pos, q, k)
        return remote(at, at, fs.at[pos, q], fr.at[pos, q], other, z)

    @pl.loop(0, n)
    def _(q):
        for pos in range(pieces):
            arrived(held_at(pos, q, k), wr.at[pos, q])
            share_copy(pos, q).start()

    @pl.loop(0, n)
    def _(q):
        for pos in range(pieces):
            share_copy(pos, q).wait()

    CB = 256
    UB = 512
    per = D // UB

    def spread(block, width):
        return jnp.concatenate([block] * (width // 128), axis=1)

    def hop_forward(b, part):
        at, col = rows(b, MT), pl.ds(part * HW, HW)
        return remote(
            s_out.at[at, col], s_in.at[at, col], hfs.at[b, part], hfr.at[b, part], next_s, next_z
        )

    def give_out(b):
        return (
            s_out.at[rows(b, MT)],
            r_out.at[rows(k, MT)],
            sos.at[b],
            sor.at[k],
            own_s,
            PLANES * rho + b,
            own_e == 1,
        )

    def give_grad(b):
        return (
            g_out.at[rows(b, MT)],
            r_grad.at[rows(k, MT)],
            sgs.at[b],
            sgr.at[k],
            own_s,
            PLANES * rho + b,
            own_e == 0,
        )

    halves = ((xn, pxn, D // 2), (xg, pxg, D // 2), (x2, px2, D // 2), (xa, pxa, FF // 2))

    def swap_left(b, pos):
        src, dst, width = halves[pos]
        at = rows(b, MT)
        return remote(
            src.at[at, rows(1 - k, width)], dst.at[at], xs.at[pos, b], xr.at[pos, b], other, z
        )

    fulls = ((dp, pdp), (dg, pdg), (dh, pdh), (g_arr, pdm))

    def swap_right(b, pos):
        src, dst = fulls[pos]
        at = rows(b, MT)
        return remote(src.at[at], dst.at[at], ds.at[pos, b], dr.at[pos, b], other, z)

    @pl.when(jnp.logical_and(first, k == 0))
    def _():
        pl.semaphore_signal(lag_sem, inc=1, device_id=(other, z), device_id_type=MESH)

    @pl.when(jnp.logical_and(first, k == 1))
    def _():
        pl.semaphore_wait(lag_sem, 1)

    @pl.loop(0, m)
    def _(b):
        at = rows(b, MT)
        for part in range(HOPS):
            arrived(s_in.at[at, pl.ds(part * HW, HW)], hfr.at[b, part])
        stream = s_in[at, :].astype(F32)
        unit, _ = norm_parts(stream)
        normed = (unit * v1[0:1, :] + v1[1:2, :]).astype(BF16)
        xn[at, :] = normed
        bb = spread(bm[at, :], CB)
        for cb in range(D // CB):
            col = slice(cb * CB, (cb + 1) * CB)
            parts = []
            for group in range(3):
                wcol = slice(group * D + cb * CB, group * D + (cb + 1) * CB)
                p = jnp.dot(normed, w[group, :, col], preferred_element_type=F32) + bi[0:1, wcol]
                y1 = bb * pltpu.roll(p, 1, 0)
                y2 = bb * pltpu.roll(y1, 1, 0)
                out = ks[0:1, wcol] * p + ks[1:2, wcol] * y1 + ks[2:3, wcol] * y2
                proj[at, wcol] = p
                conv[at, wcol] = out
                parts.append(out)
            mixed = parts[2] * parts[1]
            total = (v1[2:3, col] + taps[0:1, col]) * mixed
            moved = mixed
            for lag in range(1, lags):
                moved = bb * pltpu.roll(moved, 1, 0)
                total = total + taps[lag : lag + 1, col] * moved
            lcs[at, col] = total
            xg[at, col] = (total * parts[0]).astype(BF16)
        gated = xg[at, :]
        for cb in range(D // CB):
            col = slice(cb * CB, (cb + 1) * CB)
            mid[at, col] = (
                s_in[at, col].astype(F32)
                + jnp.dot(gated, w[3, :, col], preferred_element_type=F32)
                + v1[3:4, col]
            )
        unit, _ = norm_parts(mid[at, :])
        second = (unit * v1[4:5, :] + v1[5:6, :]).astype(BF16)
        x2[at, :] = second
        for ub in range(FF // UB):
            col = slice(ub * UB, (ub + 1) * UB)
            wcol = slice((ub % per) * UB, (ub % per + 1) * UB)
            before = (
                jnp.dot(second, w[4 + ub // per, :, wcol], preferred_element_type=F32) + bu[0:1, col]
            )
            phi = 0.5 + 0.5 * lax.erf(before * (1.0 / math.sqrt(2.0)))
            dens = jnp.exp(-0.5 * before * before) * (1.0 / math.sqrt(2.0 * math.pi))
            gpr[at, col] = phi + before * dens
            xa[at, col] = (before * phi).astype(BF16)
        for part in range(HOPS):
            col = slice(part * HW, (part + 1) * HW)
            total = mid[at, col] + v1[6:7, col]
            for q in range(wide):
                total = total + jnp.dot(
                    xa[at, q * D : (q + 1) * D], w[blocks + q, :, col], preferred_element_type=F32
                )
            s_out[at, col] = total.astype(BF16)

            @pl.when(jnp.logical_not(last))
            def _():
                hop_forward(b, part).start()

        start(*give_out(b))
        for pos in range(4):
            swap_left(b, pos).start()

    @pl.when(defers)
    def _():
        pass_rest()

    TB = 256

    @pl.loop(0, blocks + wide)
    def _(b):
        for top in range(D // TB):
            up = slice(top * TB, (top + 1) * TB)
            w[b, up, up] = w[b, up, up].T
            for low in range(top + 1, D // TB):
                down = slice(low * TB, (low + 1) * TB)
                one, two = w[b, up, down], w[b, down, up]
                w[b, up, down] = two.T
                w[b, down, up] = one.T

    def hop_back(b):
        at = rows(b, MT)
        return remote(g_out.at[at], g_arr.at[at], hbs.at[b], hbr.at[b], prev_s, prev_z)

    @pl.when(jnp.logical_and(last, k == 0))
    def _():
        pl.semaphore_signal(lag_sem, inc=1, device_id=(other, z), device_id_type=MESH)

    @pl.when(jnp.logical_and(last, k == 1))
    def _():
        pl.semaphore_wait(lag_sem, 1)

    @pl.loop(0, m)
    def _(b):
        at = rows(b, MT)
        arrived(g_arr.at[at], hbr.at[b])
        swap_right(b, 3).start()
        low = g_arr[at, :]
        grad = low.astype(F32)
        a1[6] += fold(grad)
        for ub in range(FF // UB):
            col = slice(ub * UB, (ub + 1) * UB)
            wcol = slice((ub % per) * UB, (ub % per + 1) * UB)
            inner = (
                jnp.dot(low, w[blocks + ub // per, :, wcol], preferred_element_type=F32)
                * gpr[at, col]
            )
            abu[:, col] += fold(inner)
            dh[at, col] = inner.astype(BF16)
        swap_right(b, 2).start()

        def times(left, begin, count):
            parts = []
            for cb in range(D // CB):
                col = slice(cb * CB, (cb + 1) * CB)
                parts.append(
                    sum(
                        jnp.dot(
                            left[at, q * D : (q + 1) * D],
                            w[begin + q, :, col],
                            preferred_element_type=F32,
                        )
                        for q in range(count)
                    )
                )
            return jnp.concatenate(parts, axis=1)

        grad2 = times(dh, 4, wide)
        unit, rate = norm_parts(mid[at, :])
        a1[4] += fold(grad2 * unit)
        a1[5] += fold(grad2)
        middle = grad + norm_back(grad2, v1[4:5, :], unit, rate)
        a1[3] += fold(middle)
        mid[at, :] = middle
        low = middle.astype(BF16)
        dg[at, :] = low
        swap_right(b, 1).start()
        bb = bm[at, :]
        bb = spread(pltpu.roll(bb, MT - 1, 0), CB)
        for cb in range(D // CB):
            col = slice(cb * CB, (cb + 1) * CB)
            gg = jnp.dot(low, w[3, :, col], preferred_element_type=F32)
            cols = [slice(g * D + cb * CB, g * D + (cb + 1) * CB) for g in range(3)]
            c_out, c_in, c_val = (conv[at, item] for item in cols)
            d_out = gg * lcs[at, col]
            moved = gg * c_out
            mixed = c_in * c_val
            direct = fold(moved * mixed)
            a1[2, :, col] += direct
            atp[0, :, col] += direct
            total = (v1[2:3, col] + taps[0:1, col]) * moved
            for lag in range(1, lags):
                moved = bb * pltpu.roll(moved, MT - 1, 0)
                total = total + taps[lag : lag + 1, col] * moved
                atp[lag, :, col] += fold(moved * mixed)
            for item, piece in zip(cols, (d_out, total * c_val, total * c_in)):
                z1 = bb * pltpu.roll(piece, MT - 1, 0)
                z2 = bb * pltpu.roll(z1, MT - 1, 0)
                p = proj[at, item]
                whole = ks[0:1, item] * piece + ks[1:2, item] * z1 + ks[2:3, item] * z2
                aks[0, :, item] += fold(p * piece)
                aks[1, :, item] += fold(p * z1)
                aks[2, :, item] += fold(p * z2)
                abi[:, item] += fold(whole)
                dp[at, item] = whole.astype(BF16)
        swap_right(b, 0).start()
        grad1 = times(dp, 0, 3)
        unit, rate = norm_parts(s_in[at, :].astype(F32))
        a1[0] += fold(grad1 * unit)
        a1[1] += fold(grad1)
        g_out[at, :] = (mid[at, :] + norm_back(grad1, v1[0:1, :], unit, rate)).astype(BF16)

        @pl.when(jnp.logical_not(first))
        def _():
            hop_back(b).start()

        start(*give_grad(b))

    @pl.loop(0, m)
    def _(b):
        for pos in range(4):
            swap_left(b, pos).wait()
            swap_right(b, pos).wait()

    def made_at(pos, q):
        if pos < blocks:
            return pos, q * dn
        return blocks + div(q * fn, D), rem(q * fn, D)

    def home_at(e, copy, pos):
        if pos < 3:
            return g_in_w.at[e, copy, :, pl.ds(pos * D, D)]
        if pos == 3:
            return g_out_w.at[e, copy]
        if pos < blocks:
            return g_up_w.at[e, copy, :, pl.ds((pos - 4) * D, D)]
        return g_down_w.at[e, copy]

    def back_at(group, copy, pos):
        return back.at[group, copy, pos] if pos < blocks else back_down.at[group, copy]

    own_group = div(layer, C)
    relayed = own_group >= 2

    def made(pos, half):
        q = k * (n // 2) + half
        block, begin = made_at(pos, q)
        share = dn if pos < blocks else fn
        return q, w.at[block, pl.ds(pl.multiple_of(begin, share), share)]

    def relay_copy(pos, half):
        q, src = made(pos, half)
        to = jnp.maximum(own_group - 2, 0)
        return (
            src,
            back_at(to, rho, pos),
            gs.at[pos, half],
            br.at[to, rho, pos],
            2 * c + rem(own_s, 2),
            q,
            relayed,
        )

    def direct_copy(pos, half):
        q, src = made(pos, half)
        return (
            src,
            home_at(own_e, rho, pos),
            gs.at[pos, half],
            gr.at[pos, own_e, rho],
            own_s,
            q,
            jnp.logical_not(relayed),
        )

    def home_copy(group, copy, pos):
        lay = layer_of(c, jnp.int32((group + 3) % PLANES), C)
        to_s, e = div(lay, 2), rem(lay, 2)
        mine = rem(to_s, 2) == k
        return mine, (
            back_at(group, copy, pos),
            home_at(e, copy, pos),
            bs.at[group, copy, pos],
            gr.at[pos, e, copy],
            to_s,
            z,
        )

    RB = min(256, dn)

    for pos in reversed(range(pieces)):

        @pl.loop(0, n // 2)
        def _(turn):
            half = rem(turn + c, n // 2)
            q = k * (n // 2) + half
            kind = 0 if pos < 3 else 1 if pos == 3 else 2 if pos < blocks else 3
            left = (xn, xg, x2, xa)[kind]
            left2 = (pxn, pxg, px2, pxa)[kind]
            right, right2 = fulls[kind]
            begin_col = (pos, 0, pos - 4, 0)[kind] * D
            col = slice(begin_col, begin_col + D)
            share = dn if pos < blocks else fn
            block, begin = made_at(pos, q)

            @pl.loop(0, share // RB)
            def _(t):
                mine = left[:, pl.ds(pl.multiple_of(q * share + t * RB, RB), RB)]
                theirs = left2[:, pl.ds(pl.multiple_of(half * share + t * RB, RB), RB)]
                at = pl.ds(pl.multiple_of(begin + t * RB, RB), RB)
                w[block, at, :] = (
                    dot_tokens(mine, right[:, col]) + dot_tokens(theirs, right2[:, col])
                ).astype(BF16)

            start(*relay_copy(pos, half))
            start(*direct_copy(pos, half))

    def total(value):
        return jnp.sum(value, axis=0, keepdims=True)

    dt = jnp.concatenate([total(atp[lag]) for lag in range(lags)], axis=0) * decay[...]
    one, cos1, two, cos2 = (fstate[index] for index in range(4))
    d_tw = dot_tokens(two[:, 0:units], dt, HIGH)
    tw2 = jnp.concatenate([tw[...], jnp.zeros_like(tw)], axis=0)
    d_two = (
        lax.dot_general(dt, tw2, (((1,), (1,)), ((), ())), precision=HIGH, preferred_element_type=F32)
        * cos2
    )
    d_deep = dot_tokens(d_two, one, HIGH)
    d_one = jnp.dot(d_two, ft[:, 128:256], precision=HIGH, preferred_element_type=F32) * cos1
    d_one = jnp.where(lane < units, d_one, 0.0)
    fgrad[:, 0:128] = dot_tokens(d_one, table[...], HIGH)
    fgrad[:, 128:256] = d_deep
    vec = [total(a1[index]) for index in range(7)]
    bias, bias_up = total(abi[...]), total(abu[...])
    taps3 = [total(aks[tap]) for tap in range(3)]
    for q in range(n):
        at = slice(q * dn, (q + 1) * dn)
        for index in range(7):
            sgrad[q, index : index + 1, :] = vec[index][:, at]
        for r in range(3):
            wide_at = slice((3 * q + r) * dn, (3 * q + r + 1) * dn)
            sgrad[q, 7 + r : 8 + r, :] = bias[:, wide_at]
            for tap in range(3):
                row = 10 + 3 * tap + r
                sgrad[q, row : row + 1, :] = taps3[tap][:, wide_at]
        for r in range(wide):
            wide_at = slice((wide * q + r) * dn, (wide * q + r + 1) * dn)
            sgrad[q, 19 + r : 20 + r, :] = bias_up[:, wide_at]
        sgrad[q, SMALL : SMALL + units, :] = d_tw[:, at]

    def vector_copies(q):
        slot = 2 * rho + k
        yield (sgrad.at[q], g_small.at[own_e, slot], vs.at[0, q], vr.at[0, own_e, slot], own_s, q)
        yield (
            fgrad.at[rows(q, un)],
            g_filt.at[own_e, slot],
            vs.at[1, q],
            vr.at[1, own_e, slot],
            own_s,
            q,
        )

    @pl.loop(0, n)
    def _(q):
        for copy in vector_copies(q):
            start(*copy)

    for group in (1, 0):
        for copy in range(R):
            for pos in reversed(range(pieces)):
                mine, args = home_copy(group, copy, pos)

                @pl.when(mine)
                def _():
                    arrived(back_at(group, copy, pos), br.at[group, copy, pos])

                start(*args, mine)

    for copy in token_copies():
        sent(*copy)
    for copy in column_copies():
        sent(*copy)
    for copy in small_copies():
        sent(*copy)
    for group in range(PLANES):
        for pos in range(pieces):
            for copy in plane_copies(group, pos):
                sent(*copy)

    @pl.loop(0, m)
    def _(b):
        @pl.when(jnp.logical_not(last))
        def _():
            for part in range(HOPS):
                hop_forward(b, part).wait_send()

        @pl.when(jnp.logical_not(first))
        def _():
            hop_back(b).wait_send()

        sent(*give_out(b))
        sent(*give_grad(b))

    @pl.loop(0, n)
    def _(q):
        for copy in vector_copies(q):
            sent(*copy)

    @pl.loop(0, n // 2)
    def _(half):
        for pos in range(pieces):
            sent(*relay_copy(pos, half))
            sent(*direct_copy(pos, half))

    for group in range(2):
        for copy in range(R):
            for pos in range(pieces):
                mine, args = home_copy(group, copy, pos)
                sent(*args, mine)

    for core in range(2):
        arrived(r_out.at[rows(jnp.int32(core), MT)], sor.at[core])
        arrived(r_grad.at[rows(jnp.int32(core), MT)], sgr.at[core])

    @pl.loop(0, 2)
    def _(e):
        for slot in range(2 * R):
            arrived(g_small.at[e, slot], vr.at[0, e, slot])
            arrived(g_filt.at[e, slot], vr.at[1, e, slot])
        for copy in range(R):
            for pos in range(pieces):
                arrived(home_at(e, copy, pos), gr.at[pos, e, copy])


def constants(length, width, lags):
    steps = np.arange(lags, dtype=np.float32)
    bands = np.arange(1, 17, dtype=np.float32)
    angles = np.float32(2.0 * np.pi) * steps[:, None] * bands[None, :] / np.float32(length)
    table = np.zeros((lags, 128), np.float32)
    table[:, 0] = steps / length
    table[:, 1:17] = np.cos(angles)
    table[:, 17:33] = np.sin(angles)
    table[:, 33] = 1.0
    rates = np.exp(np.linspace(math.log(0.3), math.log(30.0), width)).astype(np.float32)
    decay = np.exp(-(steps / np.float32(length))[:, None] * rates[None, :]).astype(np.float32)
    return table, decay


def on_device(
    S,
    n,
    tokens,
    cotangent,
    lengths,
    mixer_gain,
    mixer_shift,
    input_weight,
    input_bias,
    short_kernel,
    embed_weight,
    embed_bias,
    filter_weight,
    filter_bias,
    taps_weight,
    skip_gain,
    output_weight,
    output_bias,
    feed_gain,
    feed_shift,
    up_weight,
    up_bias,
    down_weight,
    down_bias,
):
    micro, length, D = tokens.shape
    FF = up_weight.shape[-1]
    dn = mixer_gain.shape[-1]
    units = filter_weight.shape[1]
    un = units // n
    emb = embed_weight.shape[1]
    R = n // PLANES
    m = PLANES
    MT = micro * length // 2
    TT = m * MT
    lags = length // 2
    wide = FF // D

    table, decay = constants(length, D, lags)

    hbm = pl.BlockSpec(memory_space=pl.ANY)
    vmem = pl.BlockSpec(memory_space=pltpu.VMEM)
    smem = pl.BlockSpec(memory_space=pltpu.SMEM)
    dma = pltpu.SemaphoreType.DMA
    blocks = 4 + wide
    pieces = blocks + 1
    out_shape = (
        jax.ShapeDtypeStruct((2, R, dn, 3 * D), BF16),
        jax.ShapeDtypeStruct((2, R, dn, D), BF16),
        jax.ShapeDtypeStruct((2, R, dn, FF), BF16),
        jax.ShapeDtypeStruct((2, R, FF // n, D), BF16),
        jax.ShapeDtypeStruct((2, 2 * R, SMALL + units, dn), F32),
        jax.ShapeDtypeStruct((2, 2 * R, un, 256), F32),
        jax.ShapeDtypeStruct((2 * MT, D), BF16),
        jax.ShapeDtypeStruct((2 * MT, D), BF16),
        jax.ShapeDtypeStruct((PLANES, blocks, dn // 2, D), BF16),
        jax.ShapeDtypeStruct((PLANES, FF // n // 2, D), BF16),
        jax.ShapeDtypeStruct((2, R, blocks, dn, D), BF16),
        jax.ShapeDtypeStruct((2, R, FF // n, D), BF16),
    )
    V = pltpu.VMEM
    scratch = [
        V((blocks + wide, D, D), BF16),
        V((n, SMALL + units, dn), F32),
        V((2 * units, 256), F32),
        V((2, SMALL + units, dn), F32),
        V((2, un, 256), F32),
        V((MT, 128), F32),
        V((128, 128), F32),
        V((8, D), F32),
        V((8, 3 * D), F32),
        V((8, 3 * D), F32),
        V((8, FF), F32),
        V((units, D), F32),
        V((lags, D), F32),
        V((4, lags, 2 * units), F32),
        V((TT, 128), F32),
        V((TT, D), BF16),
        V((TT, D), BF16),
        V((TT, D), BF16),
        V((TT, D), BF16),
        V((TT, D), BF16),
        V((TT, D), BF16),
        V((TT, D), BF16),
        V((TT, FF), BF16),
        V((TT, 3 * D), F32),
        V((TT, 3 * D), F32),
        V((TT, D), F32),
        V((TT, FF), F32),
        V((TT, D), F32),
        V((TT, 3 * D), BF16),
        V((TT, D), BF16),
        V((TT, FF), BF16),
        V((TT, D // 2), BF16),
        V((TT, D // 2), BF16),
        V((TT, D // 2), BF16),
        V((TT, FF // 2), BF16),
        V((TT, 3 * D), BF16),
        V((TT, D), BF16),
        V((TT, FF), BF16),
        V((TT, D), BF16),
        V((7, 8, D), F32),
        V((8, 3 * D), F32),
        V((3, 8, 3 * D), F32),
        V((8, FF), F32),
        V((lags, 8, D), F32),
        V((n, SMALL + units, dn), F32),
        V((2 * units, 256), F32),
        dma((2, 2, pieces)),
        dma((PLANES, pieces)),
        dma((PLANES, R, pieces)),
        dma((pieces, n)),
        dma((pieces, n)),
        dma((pieces, n)),
        dma((2, 2, R, 2)),
        dma((2, n)),
        dma((PLANES,)),
        dma((PLANES,)),
        dma((HOPS,)),
        dma((1,)),
        dma((m, HOPS)),
        dma((m, HOPS)),
        dma((m,)),
        dma((m,)),
        dma((m,)),
        dma((2,)),
        dma((m,)),
        dma((2,)),
        dma((4, m)),
        dma((4, m)),
        dma((4, m)),
        dma((4, m)),
        dma((pieces, n // 2)),
        dma((pieces, 2, R)),
        dma((2, R, pieces)),
        dma((2, R, pieces)),
        dma((2, n)),
        dma((2, 2, 2 * R)),
        pltpu.SemaphoreType.REGULAR,
    ]
    size = (S, n, R, D, FF, m, MT, lags, units, length)
    gi, go, gu, gd, gsm, gft, r_out, r_grad, *_ = pl.pallas_call(
        functools.partial(kernel, size),
        out_shape=out_shape,
        in_specs=[hbm] * 6 + [smem] + [vmem] * 11,
        out_specs=(hbm,) * 12,
        scratch_shapes=scratch,
        compiler_params=pltpu.CompilerParams(
            collective_id=0, has_side_effects=True, vmem_limit_bytes=62 << 20
        ),
        name="window",
    )(
        tokens.reshape(micro * length, D),
        cotangent.reshape(micro * length, D),
        input_weight,
        output_weight,
        up_weight,
        down_weight,
        lengths,
        jnp.stack(
            [mixer_gain, mixer_shift, skip_gain, output_bias, feed_gain, feed_shift, down_bias]
        ),
        input_bias,
        short_kernel,
        up_bias,
        taps_weight,
        embed_weight,
        embed_bias,
        filter_weight,
        filter_bias,
        jnp.asarray(decay),
        jnp.asarray(table),
    )

    def whole(piece):
        return jnp.sum(piece.astype(F32), axis=1)

    vectors = jnp.sum(gsm, axis=1)
    nets = jnp.sum(gft, axis=1)

    def take(begin, count=1):
        return vectors[:, begin : begin + count].reshape(2, count * dn)

    def stream(piece):
        return piece.astype(F32).reshape(1, micro, length, D)

    return (
        stream(r_out),
        stream(r_grad),
        take(0),
        take(1),
        whole(gi),
        take(7, 3),
        vectors[:, 10:19].reshape(2, 3, 3 * dn),
        nets[:, :, 0:emb].transpose(0, 2, 1),
        nets[:, :, emb],
        nets[:, :, 128 : 128 + units].transpose(0, 2, 1),
        nets[:, :, 128 + units],
        vectors[:, SMALL:],
        take(2),
        whole(go),
        take(3),
        take(4),
        take(5),
        whole(gu),
        take(19, wide),
        whole(gd),
        take(6),
    )


def solution(mesh):
    S, n = mesh.shape["section"], mesh.shape["dp"]
    vector, matrix, columns = P("section", "dp"), P("section", "dp", None), P("section", None, "dp")
    weights = (
        vector,
        vector,
        matrix,
        vector,
        columns,
        columns,
        vector,
        columns,
        vector,
        columns,
        vector,
        matrix,
        vector,
        vector,
        vector,
        matrix,
        vector,
        matrix,
        vector,
    )
    rows = P("section", "dp", None, None)
    return jax.shard_map(
        functools.partial(on_device, S, n),
        mesh=mesh,
        in_specs=(P("dp", None, None), P("dp", None, None), P("dp", None)) + weights,
        out_specs=(rows, rows) + weights,
        check_vma=False,
    )
```

time: 5280 us -> 982 us (0.19)
  waiting for transfers between devices: 3680 us -> 0 us
  Pallas kernels: 0 us -> 944 us
  matrix products: 401 us -> 0 us
  starting transfers between devices: 364 us -> 0 us
  other arithmetic: 336 us -> 20.8 us
  local copies, waits for them, and re-layouts: 259 us -> 15.7 us
  blocking collectives: 183 us -> 0 us
    reduce_scatter x5 -> x0, waiting for transfers between devices: 1700 us -> none  [the longest x1 556 us: on_device(): lax.psum_scatter(full_grads[15], 'dp', scatter_dimension=1, tiled=True)]
    ppermute x22 -> x0, waiting for transfers between devices: 1120 us -> none  [from_behind(): lax.ppermute(value, axis, [(source, source + steps) for source in range(i...]
    pallas_call x0 -> x1, Pallas kernels: none -> 944 us  [on_device(): pl.pallas_call(functools.partial(kernel, size), out_shape=out_shape, in_s...]
    all_gather x4 -> x0, waiting for transfers between devices: 671 us -> none  [the longest x1 276 us: on_device(): lax.all_gather(up_weight, 'dp', axis=1, tiled=True)]
    dot_general x108 -> x0, matrix products: 401 us -> none  [the longest x12 95.6 us: layer_forward(): jnp.dot(activated, down_weight, preferred_element_type=jnp.float32)]
    ppermute x22 -> x0, starting transfers between devices: 363 us -> none  [from_behind(): lax.ppermute(value, axis, [(source, source + steps) for source in range(i...]
    unnamed x33 -> x0, waiting for transfers between devices: 184 us -> none
    all_gather x15 -> x0, blocking collectives: 167 us -> none  [the longest x1 23.5 us: on_device(): lax.all_gather(taps_weight, 'dp', axis=2, tiled=True)]
  transfers between devices with their start and end apart: 43 -> 0, of which waited for: 37 -> 0; matrix products, arithmetic and copies ran while one was open for 3% -> 0% of each run, Pallas kernels for 0% -> 0%
where the time goes in v1:
time: 982 us; the launch traced here: 981 us
  Pallas kernels  944 us (96%)
  other arithmetic  20.8 us (2%)
  local copies, waits for them, and re-layouts  15.7 us (2%)
    pallas_call x1, Pallas kernels, on_device(): pl.pallas_call(functools.partial(kernel, size), out_shape=out_shape, in_s...  944 us

profile of v1, /device:TPU:25, one launch (start us, length us, event | category | flops | bytes accessed | tf_op | source)
XLA Modules:
  0.0 981.1 jit_solution(1876074446203843720)
XLA Ops:
  0.7 0.7 constant_dynamic-update-slice_fusion.6
  1.3 0.7 constant_dynamic-update-slice_fusion.5
  2.0 0.7 constant_dynamic-update-slice_fusion.4
  2.7 0.7 constant_dynamic-update-slice_fusion.3
  3.4 0.7 constant_dynamic-update-slice_fusion.2
  4.1 0.7 constant_dynamic-update-slice_fusion.1
  4.8 0.7 constant_dynamic-update-slice_fusion.vectors
  5.5 1.3 copy.57.short_kernel
  6.8 1.4 copy.58.embed_weight
  8.2 1.4 copy.59.filter_weight
  9.6 0.0 copy-done.3
  9.6 943.8 %window.1 = (bf16[2,1,256,3072]{3,2,1,0:T(8,128)(2,1)}, bf16[2,1,256,1024]{3,2,1,0:T(8,128)(2,1)}, bf16[2,1,256,4096]{3,2,1,0:T(8,128)(2,1)}, bf16[2,1,1024,1024...) custom-call(bf16[128,1024]{1,0:T(8,128)(2,1)} %bitcast.57, ...), custom_call_target="tpu_custom_call" | custom-call | tf_op jit(solution)/shard_map/window/pallas_call | solution.py:1116
  953.4 0.0 copy-start.2
  953.4 1.0 reduce_sum.53
  954.4 1.0 reduce_sum.50
  955.4 0.7 slice_reduce_fusion
  956.2 0.6 copy.68
  956.8 0.6 copy.69
  957.4 0.6 copy_bitcast_fusion
  958.0 0.6 copy.77
  958.6 0.6 copy_bitcast_fusion.2
  959.2 0.6 copy_bitcast_fusion.4
  959.7 0.6 slice_bitcast_fusion
  960.3 0.6 slice_bitcast_fusion.1
  961.0 0.7 slice.68
  961.6 0.6 copy.60
  962.3 1.8 convert.7
  964.0 1.8 convert.6
  965.8 2.8 bitcast_convert_fusion.3
  968.6 3.5 bitcast_convert_fusion.2
  972.1 4.5 bitcast_convert_fusion.1
  976.6 4.4 bitcast_convert_fusion
  (11 shorter events, 0.0 us)
Async XLA Ops:
  5.5 4.1 copy-start.3
  953.4 15.2 %copy-start.2 = (bf16[2,1,256,3072]{3,2,1,0:T(8,128)(2,1)S(1)}, bf16[2,1,256,3072]{3,2,1,0:T(8,128)(2,1)}, u32[]{:S(2)}) copy-start(bf16[2,1,256,3072]{3,2,1,0:T(8,128)(2,1)} %get-tuple-element.32) | copy-start | bytes 9437188
  968.6 3.5 copy-start.1
  972.1 4.5 copy-start

commit v2 on v1

--- a/solution.py
+++ b/solution.py
@@ -16,7 +16,7 @@
 PLANES = 4
 SMALL = 32
 HIGH = lax.Precision.HIGHEST
-HOPS = 4
+HOPS = 2
 
 
 def div(a, b):
@@ -91,6 +91,12 @@
 
 def dot_right(left, right):
     return lax.dot_general(left, right, (((1,), (1,)), ((), ())), preferred_element_type=F32)
+
+
+def dot_rows(left, right):
+    count = left.shape[0]
+    twice = jnp.concatenate([left, left], axis=0)
+    return jnp.dot(twice, right, preferred_element_type=F32)[0:count]
 
 
 def dot_tokens(left, right, precision=None):
@@ -108,7 +114,13 @@
     up_w,
     down_w,
     lengths,
-    vectors,
+    mixer_gain,
+    mixer_shift,
+    skip_gain,
+    output_bias,
+    feed_gain,
+    feed_shift,
+    down_bias,
     input_bias,
     short_kernel,
     up_bias,
@@ -390,8 +402,9 @@
         own_mask[r * length : (r + 1) * length, :] = jnp.where(begins, 0.0, 1.0)
 
     own_sm[...] = jnp.zeros_like(own_sm)
-    for index in range(7):
-        own_sm[:, index, :] = vectors[index, :, :].astype(F32)
+    shares = (mixer_gain, mixer_shift, skip_gain, output_bias, feed_gain, feed_shift, down_bias)
+    for index, share in enumerate(shares):
+        own_sm[:, index, :] = share[...].astype(F32)
     wide_bias, wide_up = input_bias[...].astype(F32), up_bias[...].astype(F32)
     for r in range(3):
         own_sm[:, 7 + r, :] = wide_bias[:, r * dn : (r + 1) * dn]
@@ -572,7 +585,7 @@
             parts = []
             for group in range(3):
                 wcol = slice(group * D + cb * CB, group * D + (cb + 1) * CB)
-                p = jnp.dot(normed, w[group, :, col], preferred_element_type=F32) + bi[0:1, wcol]
+                p = dot_rows(normed, w[group, :, col]) + bi[0:1, wcol]
                 y1 = bb * pltpu.roll(p, 1, 0)
                 y2 = bb * pltpu.roll(y1, 1, 0)
                 out = ks[0:1, wcol] * p + ks[1:2, wcol] * y1 + ks[2:3, wcol] * y2
@@ -592,7 +605,7 @@
             col = slice(cb * CB, (cb + 1) * CB)
             mid[at, col] = (
                 s_in[at, col].astype(F32)
-                + jnp.dot(gated, w[3, :, col], preferred_element_type=F32)
+                + dot_rows(gated, w[3, :, col])
                 + v1[3:4, col]
             )
         unit, _ = norm_parts(mid[at, :])
@@ -602,7 +615,7 @@
             col = slice(ub * UB, (ub + 1) * UB)
             wcol = slice((ub % per) * UB, (ub % per + 1) * UB)
             before = (
-                jnp.dot(second, w[4 + ub // per, :, wcol], preferred_element_type=F32) + bu[0:1, col]
+                dot_rows(second, w[4 + ub // per, :, wcol]) + bu[0:1, col]
             )
             phi = 0.5 + 0.5 * lax.erf(before * (1.0 / math.sqrt(2.0)))
             dens = jnp.exp(-0.5 * before * before) * (1.0 / math.sqrt(2.0 * math.pi))
@@ -612,9 +625,7 @@
             col = slice(part * HW, (part + 1) * HW)
             total = mid[at, col] + v1[6:7, col]
             for q in range(wide):
-                total = total + jnp.dot(
-                    xa[at, q * D : (q + 1) * D], w[blocks + q, :, col], preferred_element_type=F32
-                )
+                total = total + dot_rows(xa[at, q * D : (q + 1) * D], w[blocks + q, :, col])
             s_out[at, col] = total.astype(BF16)
 
             @pl.when(jnp.logical_not(last))
@@ -666,7 +677,7 @@
             col = slice(ub * UB, (ub + 1) * UB)
             wcol = slice((ub % per) * UB, (ub % per + 1) * UB)
             inner = (
-                jnp.dot(low, w[blocks + ub // per, :, wcol], preferred_element_type=F32)
+                dot_rows(low, w[blocks + ub // per, :, wcol])
                 * gpr[at, col]
             )
             abu[:, col] += fold(inner)
@@ -679,11 +690,7 @@
                 col = slice(cb * CB, (cb + 1) * CB)
                 parts.append(
                     sum(
-                        jnp.dot(
-                            left[at, q * D : (q + 1) * D],
-                            w[begin + q, :, col],
-                            preferred_element_type=F32,
-                        )
+                        dot_rows(left[at, q * D : (q + 1) * D], w[begin + q, :, col])
                         for q in range(count)
                     )
                 )
@@ -703,7 +710,7 @@
         bb = spread(pltpu.roll(bb, MT - 1, 0), CB)
         for cb in range(D // CB):
             col = slice(cb * CB, (cb + 1) * CB)
-            gg = jnp.dot(low, w[3, :, col], preferred_element_type=F32)
+            gg = dot_rows(low, w[3, :, col])
             cols = [slice(g * D + cb * CB, g * D + (cb + 1) * CB) for g in range(3)]
             c_out, c_in, c_val = (conv[at, item] for item in cols)
             d_out = gg * lcs[at, col]
@@ -1116,7 +1123,7 @@
     gi, go, gu, gd, gsm, gft, r_out, r_grad, *_ = pl.pallas_call(
         functools.partial(kernel, size),
         out_shape=out_shape,
-        in_specs=[hbm] * 6 + [smem] + [vmem] * 11,
+        in_specs=[hbm] * 6 + [smem] + [vmem] * 17,
         out_specs=(hbm,) * 12,
         scratch_shapes=scratch,
         compiler_params=pltpu.CompilerParams(
@@ -1131,9 +1138,13 @@
         up_weight,
         down_weight,
         lengths,
-        jnp.stack(
-            [mixer_gain, mixer_shift, skip_gain, output_bias, feed_gain, feed_shift, down_bias]
-        ),
+        mixer_gain,
+        mixer_shift,
+        skip_gain,
+        output_bias,
+        feed_gain,
+        feed_shift,
+        down_bias,
         input_bias,
         short_kernel,
         up_bias,

time: 982 us -> 882 us (0.90)
  Pallas kernels: 944 us -> 849 us
    pallas_call x1, Pallas kernels: 944 us -> 849 us  [on_device(): pl.pallas_call(functools.partial(kernel, size), out_shape=out_shape, in_s...]
where the time goes in v2:
time: 882 us; the launch traced here: 881 us
  Pallas kernels  849 us (96%)
  other arithmetic  20.8 us (2%)
  local copies, waits for them, and re-layouts  10.9 us (1%)
    pallas_call x1, Pallas kernels, on_device(): pl.pallas_call(functools.partial(kernel, size), out_shape=out_shape, in_s...  849 us

profile of v2, /device:TPU:25, one launch (start us, length us, event | category | flops | bytes accessed | tf_op | source)
XLA Modules:
  0.0 881.4 jit_solution(1690019520068172010)
XLA Ops:
  0.7 1.3 copy.57.short_kernel
  2.0 1.4 copy.58.embed_weight
  3.4 1.4 copy.59.filter_weight
  4.8 849.0 %window.1 = (bf16[2,1,256,3072]{3,2,1,0:T(8,128)(2,1)}, bf16[2,1,256,1024]{3,2,1,0:T(8,128)(2,1)}, bf16[2,1,256,4096]{3,2,1,0:T(8,128)(2,1)}, bf16[2,1,1024,1024...) custom-call(bf16[128,1024]{1,0:T(8,128)(2,1)} %bitcast.43, ...), custom_call_target="tpu_custom_call" | custom-call | tf_op jit(solution)/shard_map/window/pallas_call | solution.py:1123
  853.7 0.0 copy-start.2
  853.7 1.0 reduce_sum.53
  854.7 1.0 reduce_sum.50
  855.8 0.7 slice_reduce_fusion
  856.5 0.6 copy.68
  857.1 0.6 copy.69
  857.7 0.6 copy_bitcast_fusion
  858.3 0.6 copy.77
  858.9 0.6 copy_bitcast_fusion.2
  859.5 0.6 copy_bitcast_fusion.4
  860.1 0.6 slice_bitcast_fusion
  860.7 0.6 slice_bitcast_fusion.1
  861.3 0.7 slice.68
  862.0 0.6 copy.60
  862.6 1.8 convert.7
  864.4 1.8 convert.6
  866.2 2.8 bitcast_convert_fusion.3
  869.0 0.0 copy-done.2
  869.0 0.0 copy-start.1
  869.0 3.5 bitcast_convert_fusion.2
  872.5 0.0 copy-done.1
  872.5 0.0 copy-start
  872.5 4.5 bitcast_convert_fusion.1
  877.0 0.0 copy-done
  877.0 4.4 bitcast_convert_fusion
  (5 shorter events, 0.0 us)
Async XLA Ops:
  853.7 15.2 %copy-start.2 = (bf16[2,1,256,3072]{3,2,1,0:T(8,128)(2,1)S(1)}, bf16[2,1,256,3072]{3,2,1,0:T(8,128)(2,1)}, u32[]{:S(2)}) copy-start(bf16[2,1,256,3072]{3,2,1,0:T(8,128)(2,1)} %get-tuple-element.32) | copy-start | bytes 9437188
  869.0 3.5 copy-start.1
  872.5 4.5 copy-start

commit v3 on v2

--- a/solution.py
+++ b/solution.py
@@ -442,19 +442,12 @@
             def _():
                 pass_on(group, pos)
 
-    defers = layer == C - 1
-
-    def pass_rest():
-        for pos in range(pieces):
-            for near, group in ((1, 3), (2, 2)):
-
-                @pl.when(plane != near)
-                def _():
-                    pass_on(group, pos)
-
-    @pl.when(jnp.logical_not(defers))
-    def _():
-        pass_rest()
+    for pos in range(pieces):
+        for near, group in ((1, 3), (2, 2)):
+
+            @pl.when(plane != near)
+            def _():
+                pass_on(group, pos)
 
     @pl.loop(0, n)
     def _(q):
@@ -635,10 +628,6 @@
         start(*give_out(b))
         for pos in range(4):
             swap_left(b, pos).start()
-
-    @pl.when(defers)
-    def _():
-        pass_rest()
 
     TB = 256
 

time: 882 us -> 877 us (level)
  no operation moved by 1% of the time
where the time goes in v3:
time: 877 us; the launch traced here: 876 us
  Pallas kernels  844 us (96%)
  other arithmetic  20.8 us (2%)
  local copies, waits for them, and re-layouts  10.9 us (1%)
    pallas_call x1, Pallas kernels, on_device(): pl.pallas_call(functools.partial(kernel, size), out_shape=out_shape, in_s...  844 us

profile of v3, /device:TPU:25, one launch (start us, length us, event | category | flops | bytes accessed | tf_op | source)
XLA Modules:
  0.0 876.3 jit_solution(4479035932519938840)
XLA Ops:
  0.7 1.3 copy.57.short_kernel
  2.0 1.4 copy.58.embed_weight
  3.4 1.4 copy.59.filter_weight
  4.8 843.8 %window.1 = (bf16[2,1,256,3072]{3,2,1,0:T(8,128)(2,1)}, bf16[2,1,256,1024]{3,2,1,0:T(8,128)(2,1)}, bf16[2,1,256,4096]{3,2,1,0:T(8,128)(2,1)}, bf16[2,1,1024,1024...) custom-call(bf16[128,1024]{1,0:T(8,128)(2,1)} %bitcast.43, ...), custom_call_target="tpu_custom_call" | custom-call | tf_op jit(solution)/shard_map/window/pallas_call | solution.py:1112
  848.6 0.0 copy-start.2
  848.6 1.0 reduce_sum.53
  849.6 1.0 reduce_sum.50
  850.7 0.7 slice_reduce_fusion
  851.4 0.6 copy.68
  852.0 0.6 copy.69
  852.6 0.6 copy_bitcast_fusion
  853.2 0.6 copy.77
  853.8 0.6 copy_bitcast_fusion.2
  854.4 0.6 copy_bitcast_fusion.4
  855.0 0.6 slice_bitcast_fusion
  855.6 0.6 slice_bitcast_fusion.1
  856.2 0.7 slice.68
  856.9 0.6 copy.60
  857.5 1.8 convert.7
  859.3 1.8 convert.6
  861.1 2.8 bitcast_convert_fusion.3
  863.8 0.0 copy-done.2
  863.8 0.0 copy-start.1
  863.8 3.5 bitcast_convert_fusion.2
  867.4 0.0 copy-done.1
  867.4 0.0 copy-start
  867.4 4.5 bitcast_convert_fusion.1
  871.8 0.0 copy-done
  871.8 4.4 bitcast_convert_fusion
  (5 shorter events, 0.0 us)
Async XLA Ops:
  848.6 15.2 %copy-start.2 = (bf16[2,1,256,3072]{3,2,1,0:T(8,128)(2,1)S(1)}, bf16[2,1,256,3072]{3,2,1,0:T(8,128)(2,1)}, u32[]{:S(2)}) copy-start(bf16[2,1,256,3072]{3,2,1,0:T(8,128)(2,1)} %get-tuple-element.32) | copy-start | bytes 9437188
  863.8 3.5 copy-start.1
  867.4 4.5 copy-start

commit v4 on v3

--- a/solution.py
+++ b/solution.py
@@ -228,6 +228,7 @@
     wide = FF // D
     blocks = 4 + wide
     pieces = blocks + 1
+    order = (blocks,) + tuple(range(blocks))
     layers = PLANES * C
     s, z = lax.axis_index("section"), lax.axis_index("dp")
     k, c = rem(s, 2), div(s, 2)
@@ -309,7 +310,7 @@
         return down_w.at[e, pl.ds(core * fh, fh)]
 
     def column_copies():
-        for pos in range(pieces):
+        for pos in order:
             for e in range(2):
                 lay = 2 * s + e
                 to_c, group = column_of(lay, C), div(lay, C)
@@ -433,7 +434,7 @@
     atp[...] = jnp.zeros_like(atp)
     sgrad[...] = jnp.zeros_like(sgrad)
 
-    for pos in range(pieces):
+    for pos in order:
         for group in (0, 1):
             pass_on(group, pos)
         for near, group in ((1, 3), (2, 2)):
@@ -442,7 +443,7 @@
             def _():
                 pass_on(group, pos)
 
-    for pos in range(pieces):
+    for pos in order:
         for near, group in ((1, 3), (2, 2)):
 
             @pl.when(plane != near)

time: 877 us -> 874 us (level)
  no operation moved by 1% of the time
where the time goes in v4:
time: 874 us
  Pallas kernels  841 us (96%)
  other arithmetic  20.8 us (2%)
  local copies, waits for them, and re-layouts  10.9 us (1%)
    pallas_call x1, Pallas kernels, on_device(): pl.pallas_call(functools.partial(kernel, size), out_shape=out_shape, in_s...  841 us

profile of v4, /device:TPU:25, one launch (start us, length us, event | category | flops | bytes accessed | tf_op | source)
XLA Modules:
  0.0 873.7 jit_solution(17106124788167001908)
XLA Ops:
  0.7 1.3 copy.57.short_kernel
  2.0 1.4 copy.58.embed_weight
  3.4 1.4 copy.59.filter_weight
  4.8 841.3 %window.1 = (bf16[2,1,256,3072]{3,2,1,0:T(8,128)(2,1)}, bf16[2,1,256,1024]{3,2,1,0:T(8,128)(2,1)}, bf16[2,1,256,4096]{3,2,1,0:T(8,128)(2,1)}, bf16[2,1,1024,1024...) custom-call(bf16[128,1024]{1,0:T(8,128)(2,1)} %bitcast.43, ...), custom_call_target="tpu_custom_call" | custom-call | tf_op jit(solution)/shard_map/window/pallas_call | solution.py:1113
  846.0 0.0 copy-start.2
  846.1 1.0 reduce_sum.53
  847.1 1.0 reduce_sum.50
  848.1 0.7 slice_reduce_fusion
  848.8 0.6 copy.68
  849.4 0.6 copy.69
  850.1 0.6 copy_bitcast_fusion
  850.6 0.6 copy.77
  851.2 0.6 copy_bitcast_fusion.2
  851.8 0.6 copy_bitcast_fusion.4
  852.4 0.6 slice_bitcast_fusion
  853.0 0.6 slice_bitcast_fusion.1
  853.6 0.7 slice.68
  854.3 0.6 copy.60
  854.9 1.8 convert.7
  856.7 1.8 convert.6
  858.5 2.8 bitcast_convert_fusion.3
  861.3 0.0 copy-done.2
  861.3 0.0 copy-start.1
  861.3 3.5 bitcast_convert_fusion.2
  864.8 0.0 copy-done.1
  864.8 0.0 copy-start
  864.8 4.5 bitcast_convert_fusion.1
  869.3 0.0 copy-done
  869.3 4.4 bitcast_convert_fusion
  (5 shorter events, 0.0 us)
Async XLA Ops:
  846.0 15.2 %copy-start.2 = (bf16[2,1,256,3072]{3,2,1,0:T(8,128)(2,1)S(1)}, bf16[2,1,256,3072]{3,2,1,0:T(8,128)(2,1)}, u32[]{:S(2)}) copy-start(bf16[2,1,256,3072]{3,2,1,0:T(8,128)(2,1)} %get-tuple-element.32) | copy-start | bytes 9437188
  861.3 3.5 copy-start.1
  864.8 4.5 copy-start
